TPU v7x, 32 devices: a whole 2x2x4 slice. The times are simulated.
32 devices in a mesh: group: 2 (over y), slab: 4 (over z), shot: 4 (over x, core).
Axes of the slice: x: 2, y: 2, z: 4, core: 2. Of those that a mesh axis runs over, the one named last changes fastest.
Arguments:
- source_state: float32 [32, 5, 32, 512], P(('group', 'shot'), None, 'slab'), parts along dimension 0, may hold values from -6 to 6
- receiver_state: float32 [32, 5, 32, 512], P(('group', 'shot'), None, 'slab'), parts along dimension 0, may hold values from -6 to 6
- p_velocity: float32 [64, 512], P(('group', 'slab')), parts along dimension 0, may hold values from 1 to 2
- s_velocity: float32 [64, 512], P(('group', 'slab')), parts along dimension 0, may hold values from 0.4 to 0.65
- density: float32 [64, 512], P(('group', 'slab')), parts along dimension 0, may hold values from 1 to 2
- receiver_data: float32 [32, 4, 256], P(('group', 'shot')), parts along dimension 0, may hold values from -6 to 6
- source_x: int32 [32], P(('group', 'shot')), parts along dimension 0, may hold values from 0 to 31
- source_z: int32 [32], P(('group', 'shot')), parts along dimension 0, may hold values from 0 to 511
- receiver_x: int32 [512], P('group'), parts along dimension 0, may hold values from 0 to 31
- receiver_z: int32 [512], P('group'), parts along dimension 0, may hold values from 0 to 511
- offsets: int32 [64], replicated, may hold values from -32 to 32, as said below
Outputs:
- final_source: float32 [32, 5, 32, 512], P(('group', 'shot'), None, 'slab'), parts along dimension 0
- final_receiver: float32 [32, 5, 32, 512], P(('group', 'shot'), None, 'slab'), parts along dimension 0
- vp_image: float32 [128, 32, 512], P(('group', 'shot'), 'slab'), parts along dimension 0
- vs_image: float32 [128, 32, 512], P(('group', 'shot'), 'slab'), parts along dimension 0
- rho_image: float32 [128, 32, 512], P(('group', 'shot'), 'slab'), parts along dimension 0
There are 2 independent parts, one for each index of `group`. A program takes and returns all parts, laid end to end along the dimension named above; an argument that names none is the same for every part. Nothing has to cross between parts.
Inputs may be any that keep to these rules, and one draw needn't show every extreme that they name: 64 distinct offsets in increasing order; -32 and 32 are among them.
All inputs are finite; a program needn't handle non-finite values.
Results may differ from a plain program's by a relative error of at most 0.0032.
Values may be sent and summed in bfloat16 or wider, within the bound.
A program may use at most 64 MiB of HBM per device.

v0:
```python
import math

import jax
import jax.numpy as jnp
from jax import lax
from jax.sharding import PartitionSpec as P

STEPS = 4
SHIFT = 32


time_step = 0.3


def passed_along(value, axis, steps):
    count = lax.axis_size(axis)
    initial, last = (max(0, -steps), min(count, count - steps))
    return lax.ppermute(value, axis, [(source, source + steps) for source in range(initial, last)])


def from_left(rows):
    return passed_along(rows, "slab", 1)


def from_right(rows):
    return passed_along(rows, "slab", -1)


def back_z(field):
    return field - jnp.pad(field, ((0, 0), (0, 0), (0, 0), (1, 0)))[:, :, :, :-1]


def fore_z(field):
    return jnp.pad(field, ((0, 0), (0, 0), (0, 0), (0, 1)))[:, :, :, 1:] - field


def direct_window(pieces, reach):
    lower = [passed_along(pieces, "slab", distance) for distance in range(reach, 0, -1)]
    upper = [passed_along(pieces, "slab", -distance) for distance in range(1, reach + 1)]
    return jnp.concatenate(lower + [pieces] + upper, axis=2)


def shards(
    source_state,
    receiver_state,
    p_velocity,
    s_velocity,
    density,
    receiver_data,
    source_x,
    source_z,
    receiver_x,
    receiver_z,
    offsets,
):
    shots_here = source_state.shape[0]
    width = source_state.shape[2]
    depth = source_state.shape[3]
    reach = SHIFT // width
    extent = (2 * reach + 1) * width
    fields = [jnp.stack([source_state[:, index], receiver_state[:, index]]) for index in range(5)]
    velocity_x, velocity_z, stress_xx, stress_zz, stress_xz = fields
    buoyancy = 1.0 / density
    shear = density * s_velocity * s_velocity
    lame_first = density * (p_velocity * p_velocity - 2.0 * s_velocity * s_velocity)
    modulus = lame_first + 2.0 * shear
    signs = jnp.array([time_step, -time_step], jnp.float32).reshape(2, 1, 1, 1)
    x_cells = lax.axis_index("slab") * width + jnp.arange(width, dtype=jnp.int32)
    z_cells = jnp.arange(depth, dtype=jnp.int32)
    source_mask = (
        (x_cells[None, :, None] == source_x[:, None, None])
        & (z_cells[None, None, :] == source_z[:, None, None])
    ).astype(jnp.float32)
    place_x = (receiver_x[:, None] == x_cells[None, :]).astype(jnp.float32)
    place_z = (receiver_z[:, None] == z_cells[None, :]).astype(jnp.float32)
    source_list, window_list = ([], [])
    for step_index in range(STEPS):
        edge_xx = from_left(stress_xx[:, :, width - 1 :])
        edge_xz = from_right(stress_xz[:, :, :1])
        back_xx = stress_xx - jnp.concatenate([edge_xx, stress_xx[:, :, :-1]], axis=2)
        fore_xz = jnp.concatenate([stress_xz[:, :, 1:], edge_xz], axis=2) - stress_xz
        velocity_x = velocity_x + signs * buoyancy * (back_xx + back_z(stress_xz))
        velocity_z = velocity_z + signs * buoyancy * (fore_xz + fore_z(stress_zz))
        edge_vz = from_left(velocity_z[:, :, width - 1 :])
        edge_vx = from_right(velocity_x[:, :, :1])
        stretch = jnp.concatenate([velocity_x[:, :, 1:], edge_vx], axis=2) - velocity_x
        squeeze = back_z(velocity_z)
        slide_x = velocity_z - jnp.concatenate([edge_vz, velocity_z[:, :, :-1]], axis=2)
        slide_z = fore_z(velocity_x)
        stress_xx = stress_xx + signs * (modulus * stretch + lame_first * squeeze)
        stress_zz = stress_zz + signs * (lame_first * stretch + modulus * squeeze)
        stress_xz = stress_xz + signs * shear * (slide_x + slide_z)
        rotation = slide_z[1] - slide_x[1]
        wavelet = 2.0 * math.cos(1.3 * step_index + 0.4)
        source_add = wavelet * source_mask
        spread = receiver_data[:, step_index, :][:, :, None] * place_x[None]
        receiver_add = jnp.einsum("srx,rz->sxz", spread, place_z, precision=lax.Precision.HIGHEST)
        inject = jnp.stack([source_add, receiver_add])
        stress_xx = stress_xx + inject
        stress_zz = stress_zz + inject
        pressure = (-0.5 * (stress_xx + stress_zz)).astype(jnp.bfloat16)
        source_list.append(pressure[0])
        pieces = jnp.stack([pressure[1], rotation.astype(jnp.bfloat16)], axis=1)
        window_list.append(direct_window(pieces, reach))
    source_all = jnp.stack(source_list)
    window_all = jnp.stack(window_list)
    correlated = jnp.einsum(
        "tsxz,tscyz->cxyz", source_all, window_all, preferred_element_type=jnp.float32
    )
    scale = 1.0 / (shots_here * lax.axis_size("shot") * STEPS)
    positions = jnp.arange(extent, dtype=jnp.int32)
    local_x = jnp.arange(width, dtype=jnp.int32)
    target = local_x[None, :] + offsets[:, None] + SHIFT
    select = (positions[None, None, :] == target[:, :, None]).astype(jnp.float32)
    images = lax.psum_scatter(
        jnp.einsum("hxy,cxyz->hcxz", select, correlated, precision=lax.Precision.HIGHEST) * scale,
        "shot",
        scatter_dimension=0,
        tiled=True,
    )
    image_pp = images[:, 0]
    image_ps = images[:, 1]
    ratio = s_velocity / p_velocity
    vp_image = 2.0 * density * p_velocity * image_pp
    vs_image = 2.0 * density * s_velocity * (image_ps - 2.0 * ratio * ratio * image_pp)
    rho_image = p_velocity * p_velocity * image_pp + s_velocity * s_velocity * image_ps
    final_fields = (velocity_x, velocity_z, stress_xx, stress_zz, stress_xz)
    final_source = jnp.stack([field[0] for field in final_fields], axis=1)
    final_receiver = jnp.stack([field[1] for field in final_fields], axis=1)
    return (final_source, final_receiver, vp_image, vs_image, rho_image)


def solution(mesh):
    return jax.shard_map(
        shards,
        mesh=mesh,
        in_specs=(
            P(("group", "shot"), None, "slab", None),
            P(("group", "shot"), None, "slab", None),
            P(("group", "slab"), None),
            P(("group", "slab"), None),
            P(("group", "slab"), None),
            P(("group", "shot"), None, None),
            P(("group", "shot")),
            P(("group", "shot")),
            P("group"),
            P("group"),
            P(),
        ),
        out_specs=(
            P(("group", "shot"), None, "slab", None),
            P(("group", "shot"), None, "slab", None),
            P(("group", "shot"), "slab", None),
            P(("group", "shot"), "slab", None),
            P(("group", "shot"), "slab", None),
        ),
        check_vma=False,
    )
```

profile of v0, /device:TPU:0, one launch (start us, length us, event | category | flops | bytes accessed | tf_op | source)
XLA Modules:
  0.0 204.9 jit_solution(17401638070726877845)
XLA Ops:
  9.8 5.6 %collective-permute-start = (f32[2,4,1,512]{3,2,1,0:T(1,128)S(1)}, f32[2,4,1,512]{3,2,1,0:T(1,128)S(1)}, u32[]{:S(2)}, u32[]{:S(2)}) collective-permute-start(f32[2,4,1,512]{3,2,1,0:T(1,128)S(1)} %fusion.74), channel_id=1, source_target_pairs={{0,4},{4,8},{8,12},{1,5},{5,9},{9,13},{2,6},{6,10},{10,14},{3,7},{... | collective-permute-start | bytes 49160 | tf_op jit(solution)/shard_map/ppermute | solution.py:18
  21.7 3.9 %collective-permute-start.4 = (f32[2,4,1,512]{3,2,1,0:T(1,128)S(1)}, f32[2,4,1,512]{3,2,1,0:T(1,128)S(1)}, u32[]{:S(2)}, u32[]{:S(2)}) collective-permute-start(f32[2,4,1,512]{3,2,1,0:T(1,128)S(1)} %slice.372), channel_id=1, source_target_pairs={{0,4},{4,8},{8,12},{1,5},{5,9},{9,13},{2,6},{6,10},{10,14},{3,7},{... | collective-permute-start | bytes 49160 | tf_op jit(solution)/shard_map/ppermute | solution.py:18
  28.5 3.0 %collective-permute-done.1 = f32[2,4,1,512]{3,2,1,0:T(1,128)S(1)} collective-permute-done((f32[2,4,1,512]{3,2,1,0:T(1,128)S(1)}, f32[2,4,1,512]{3,2,1,0:T(1,128)S(1)}, u32[]{:S(2)}, u32[]{:S(2)}) %collective-permute-start.1) | collective-permute-done | bytes 16416 | tf_op jit(solution)/shard_map/ppermute | solution.py:18
  31.7 3.4 %collective-permute-start.3 = (f32[2,4,1,512]{3,2,1,0:T(1,128)S(1)}, f32[2,4,1,512]{3,2,1,0:T(1,128)S(1)}, u32[]{:S(2)}, u32[]{:S(2)}) collective-permute-start(f32[2,4,1,512]{3,2,1,0:T(1,128)S(1)} %slice.370), channel_id=1, source_target_pairs={{0,4},{4,8},{8,12},{1,5},{5,9},{9,13},{2,6},{6,10},{10,14},{3,7},{... | collective-permute-start | bytes 49160 | tf_op jit(solution)/shard_map/ppermute | solution.py:18
  35.1 1.4 collective-permute-done.3
  38.0 4.8 %collective-permute-start.8 = (f32[2,4,1,512]{3,2,1,0:T(1,128)S(1)}, f32[2,4,1,512]{3,2,1,0:T(1,128)S(1)}, u32[]{:S(2)}, u32[]{:S(2)}) collective-permute-start(f32[2,4,1,512]{3,2,1,0:T(1,128)S(1)} %slice.380), channel_id=1, source_target_pairs={{0,4},{4,8},{8,12},{1,5},{5,9},{9,13},{2,6},{6,10},{10,14},{3,7},{... | collective-permute-start | bytes 49160 | tf_op jit(solution)/shard_map/ppermute | solution.py:18
  43.5 3.0 %collective-permute-start.17 = (bf16[4,2,8,512]{3,2,0,1:T(8,128)(2,1)S(1)}, bf16[4,2,8,512]{3,2,0,1:T(8,128)(2,1)S(1)}, u32[]{:S(2)}, u32[]{:S(2)}) collective-permute-start(bf16[4,2,8,512]{3,2,0,1:T(8,128)(2,1)S(1)} %pad_maximum_fusion.8), channel_id=1, source_target_pairs={{0,12},{1,13},{2,14},{3,15},{16,28},{17,29},{18,30},{19,31}} | collective-permute-start | bytes 196616 | tf_op jit(solution)/shard_map/ppermute | solution.py:18
  46.5 1.8 collective-permute-start.18
  50.0 4.5 %collective-permute-start.7 = (f32[2,4,1,512]{3,2,1,0:T(1,128)S(1)}, f32[2,4,1,512]{3,2,1,0:T(1,128)S(1)}, u32[]{:S(2)}, u32[]{:S(2)}) collective-permute-start(f32[2,4,1,512]{3,2,1,0:T(1,128)S(1)} %slice.378), channel_id=1, source_target_pairs={{0,4},{4,8},{8,12},{1,5},{5,9},{9,13},{2,6},{6,10},{10,14},{3,7},{... | collective-permute-start | bytes 49160 | tf_op jit(solution)/shard_map/ppermute | solution.py:18
  54.6 1.9 collective-permute-start.19
  61.4 7.5 %collective-permute-start.24 = (bf16[4,2,8,512]{3,2,0,1:T(8,128)(2,1)S(1)}, bf16[4,2,8,512]{3,2,0,1:T(8,128)(2,1)S(1)}, u32[]{:S(2)}, u32[]{:S(2)}) collective-permute-start(bf16[4,2,8,512]{3,2,0,1:T(8,128)(2,1)S(1)} %pad_maximum_fusion.9), channel_id=1, source_target_pairs={{0,12},{1,13},{2,14},{3,15},{16,28},{17,29},{18,30},{19,31}} | collective-permute-start | bytes 196616 | tf_op jit(solution)/shard_map/ppermute | solution.py:18
  71.7 4.5 %collective-permute-start.12 = (f32[2,4,1,512]{3,2,1,0:T(1,128)S(1)}, f32[2,4,1,512]{3,2,1,0:T(1,128)S(1)}, u32[]{:S(2)}, u32[]{:S(2)}) collective-permute-start(f32[2,4,1,512]{3,2,1,0:T(1,128)S(1)} %slice.388), channel_id=1, source_target_pairs={{0,4},{4,8},{8,12},{1,5},{5,9},{9,13},{2,6},{6,10},{10,14},{3,7},{... | collective-permute-start | bytes 49160 | tf_op jit(solution)/shard_map/ppermute | solution.py:18
  76.3 1.4 collective-permute-done.12
  79.2 4.8 %collective-permute-start.11 = (f32[2,4,1,512]{3,2,1,0:T(1,128)S(1)}, f32[2,4,1,512]{3,2,1,0:T(1,128)S(1)}, u32[]{:S(2)}, u32[]{:S(2)}) collective-permute-start(f32[2,4,1,512]{3,2,1,0:T(1,128)S(1)} %slice.386), channel_id=1, source_target_pairs={{0,4},{4,8},{8,12},{1,5},{5,9},{9,13},{2,6},{6,10},{10,14},{3,7},{... | collective-permute-start | bytes 49160 | tf_op jit(solution)/shard_map/ppermute | solution.py:18
  84.1 1.4 collective-permute-done.11
  85.6 4.2 %collective-permute-start.15 = (f32[2,4,1,512]{3,2,1,0:T(1,128)S(1)}, f32[2,4,1,512]{3,2,1,0:T(1,128)S(1)}, u32[]{:S(2)}, u32[]{:S(2)}) collective-permute-start(f32[2,4,1,512]{3,2,1,0:T(1,128)S(1)} %slice.398), channel_id=1, source_target_pairs={{0,4},{4,8},{8,12},{1,5},{5,9},{9,13},{2,6},{6,10},{10,14},{3,7},{... | collective-permute-start | bytes 49160 | tf_op jit(solution)/shard_map/ppermute | solution.py:18
  91.3 4.5 %collective-permute-start.26 = (bf16[4,2,8,512]{3,2,0,1:T(8,128)(2,1)S(1)}, bf16[4,2,8,512]{3,2,0,1:T(8,128)(2,1)S(1)}, u32[]{:S(2)}, u32[]{:S(2)}) collective-permute-start(bf16[4,2,8,512]{3,2,0,1:T(8,128)(2,1)S(1)} %pad_maximum_fusion.9), channel_id=1, source_target_pairs={{0,4},{4,8},{8,12},{1,5},{5,9},{9,13},{2,6},{6,10},{10,14},{3,7},{... | collective-permute-start | bytes 196616 | tf_op jit(solution)/shard_map/ppermute | solution.py:18
  101.3 7.5 %collective-permute-start.31 = (bf16[4,2,8,512]{3,2,0,1:T(8,128)(2,1)S(1)}, bf16[4,2,8,512]{3,2,0,1:T(8,128)(2,1)S(1)}, u32[]{:S(2)}, u32[]{:S(2)}) collective-permute-start(bf16[4,2,8,512]{3,2,0,1:T(8,128)(2,1)S(1)} %pad_maximum_fusion.10), channel_id=1, source_target_pairs={{0,12},{1,13},{2,14},{3,15},{16,28},{17,29},{18,30},{19,31}} | collective-permute-start | bytes 196616 | tf_op jit(solution)/shard_map/ppermute | solution.py:18
  108.9 2.8 %copy.50 = bf16[4,4,8,512,1]{2,0,1,4,3:T(4,128)(2,1)} copy(bf16[4,4,8,512,1]{3,2,1,0,4:T(8,128)(2,1)S(1)} %maximum_bitcast_fusion) | data formatting | bytes 262144 | tf_op jit(solution)/shard_map/stack | solution.py:105
  113.0 2.5 %collective-permute-start.33 = (bf16[4,2,8,512]{3,2,0,1:T(8,128)(2,1)S(1)}, bf16[4,2,8,512]{3,2,0,1:T(8,128)(2,1)S(1)}, u32[]{:S(2)}, u32[]{:S(2)}) collective-permute-start(bf16[4,2,8,512]{3,2,0,1:T(8,128)(2,1)S(1)} %pad_maximum_fusion.10), channel_id=1, source_target_pairs={{0,4},{4,8},{8,12},{1,5},{5,9},{9,13},{2,6},{6,10},{10,14},{3,7},{... | collective-permute-start | bytes 196616 | tf_op jit(solution)/shard_map/ppermute | solution.py:18
  120.2 7.5 %collective-permute-start.38 = (bf16[4,2,8,512]{3,2,0,1:T(8,128)(2,1)S(1)}, bf16[4,2,8,512]{3,2,0,1:T(8,128)(2,1)S(1)}, u32[]{:S(2)}, u32[]{:S(2)}) collective-permute-start(bf16[4,2,8,512]{3,2,0,1:T(8,128)(2,1)S(1)} %pad_maximum_fusion.11), channel_id=1, source_target_pairs={{0,12},{1,13},{2,14},{3,15},{16,28},{17,29},{18,30},{19,31}} | collective-permute-start | bytes 196616 | tf_op jit(solution)/shard_map/ppermute | solution.py:18
  129.1 2.5 %collective-permute-start.40 = (bf16[4,2,8,512]{3,2,0,1:T(8,128)(2,1)S(1)}, bf16[4,2,8,512]{3,2,0,1:T(8,128)(2,1)S(1)}, u32[]{:S(2)}, u32[]{:S(2)}) collective-permute-start(bf16[4,2,8,512]{3,2,0,1:T(8,128)(2,1)S(1)} %pad_maximum_fusion.11), channel_id=1, source_target_pairs={{0,4},{4,8},{8,12},{1,5},{5,9},{9,13},{2,6},{6,10},{10,14},{3,7},{... | collective-permute-start | bytes 196616 | tf_op jit(solution)/shard_map/ppermute | solution.py:18
  134.3 1.5 collective-permute-start.43
  135.9 1.9 collective-permute-done.41
  137.8 2.2 %collective-permute-done.42 = bf16[4,2,8,512]{3,2,0,1:T(8,128)(2,1)S(1)} collective-permute-done((bf16[4,2,8,512]{3,2,0,1:T(8,128)(2,1)S(1)}, bf16[4,2,8,512]{3,2,0,1:T(8,128)(2,1)S(1)}, u32[]{:S(2)}, u32[]{:S(2)}) %collective-permute-start.42) | collective-permute-done | bytes 65568 | tf_op jit(solution)/shard_map/ppermute | solution.py:18
  140.0 3.4 %collective-permute-done.43 = bf16[4,2,8,512]{3,2,0,1:T(8,128)(2,1)S(1)} collective-permute-done((bf16[4,2,8,512]{3,2,0,1:T(8,128)(2,1)S(1)}, bf16[4,2,8,512]{3,2,0,1:T(8,128)(2,1)S(1)}, u32[]{:S(2)}, u32[]{:S(2)}) %collective-permute-start.43) | collective-permute-done | bytes 65568 | tf_op jit(solution)/shard_map/ppermute | solution.py:18
  143.5 1.4 pad_maximum_fusion
  144.8 5.5 %copy.49 = bf16[4,4,2,72,512]{3,0,1,2,4:T(4,128)(2,1)} copy(bf16[4,4,2,72,512]{4,3,1,2,0:T(8,128)(2,1)S(1)} %pad_maximum_fusion) | data formatting | bytes 4718592 | tf_op jit(solution)/shard_map/stack | solution.py:106
  150.4 8.0 %fusion.93 = f32[512,2,72,8,1]{2,3,4,1,0:T(8,128)} fusion(bf16[4,4,2,72,512]{3,0,1,2,4:T(4,128)(2,1)} %copy.49, bf16[4,4,8,512,1]{2,0,1,4,3:T(4,128)(2,1)} %copy.50), kind=kOutput, calls=%fused_computation.257 | convolution fusion | flops 18874368 | bytes 4849664 | tf_op jit(solution)/shard_map/tsxz,tscyz->cxyz/dot_general | solution.py:107
  158.4 3.5 %copy.51 = f32[512,2,72,8,1]{0,2,1,3,4:T(8,128)S(1)} copy(f32[512,2,72,8,1]{2,3,4,1,0:T(8,128)} %fusion.93) | data formatting | bytes 4718592 | tf_op jit(solution)/shard_map/tsxz,tscyz->cxyz/dot_general | solution.py:107
  161.9 2.6 %multiply_bitcast_fusion = f32[64,2,8,512]{3,0,1,2:T(8,128)} fusion(f32[512,2,72,8,1]{0,2,1,3,4:T(8,128)S(1)} %copy.51, s32[64,8]{0,1:T(8,128)S(1)} %copy-done.2), kind=kOutput, calls=%fused_computation.3 | convolution fusion | flops 453545984 | bytes 4458496 | tf_op jit(solution)/shard_map/hxy,cxyz->hcxz/dot_general | solution.py:116
  167.0 27.4 %reduce-scatter.2.cloned.1.call-done = f32[16,2,8,512]{3,0,1,2:T(8,128)} async-done(((f32[64,2,8,512]{3,0,1,2:T(8,128)}), f32[16,2,8,512]{3,0,1,2:T(8,128)}) %reduce-scatter.2.cloned.1.call-update) | async-done | bytes 524304 | tf_op jit(solution)/shard_map/reduce_scatter | solution.py:115
  (197 shorter events, 47.5 us)
Async XLA Ops:
  7.2 187.1 %reduce-scatter.2.cloned.1.call-start = ((), (), s32[]{:S(2)}) async-start(), calls=%async_computation.1 | async-start | bytes 2621440 | tf_op jit(solution)/shard_map/reduce_scatter | solution.py:115
  8.5 13.1 %collective-permute-start.2 = (f32[2,4,1,512]{3,2,1,0:T(1,128)S(1)}, f32[2,4,1,512]{3,2,1,0:T(1,128)S(1)}, u32[]{:S(2)}, u32[]{:S(2)}) collective-permute-start(f32[2,4,1,512]{3,2,1,0:T(1,128)S(1)} %fusion.73), channel_id=1, source_target_pairs={{4,0},{8,4},{12,8},{5,1},{9,5},{13,9},{6,2},{10,6},{14,10},{7,3},{... | collective-permute-start | bytes 49160 | tf_op jit(solution)/shard_map/ppermute | solution.py:18
  9.8 15.8 %collective-permute-start = (f32[2,4,1,512]{3,2,1,0:T(1,128)S(1)}, f32[2,4,1,512]{3,2,1,0:T(1,128)S(1)}, u32[]{:S(2)}, u32[]{:S(2)}) collective-permute-start(f32[2,4,1,512]{3,2,1,0:T(1,128)S(1)} %fusion.74), channel_id=1, source_target_pairs={{0,4},{4,8},{8,12},{1,5},{5,9},{9,13},{2,6},{6,10},{10,14},{3,7},{... | collective-permute-start | bytes 49160 | tf_op jit(solution)/shard_map/ppermute | solution.py:18
  27.2 7.9 %collective-permute-start.6 = (f32[2,4,1,512]{3,2,1,0:T(1,128)S(1)}, f32[2,4,1,512]{3,2,1,0:T(1,128)S(1)}, u32[]{:S(2)}, u32[]{:S(2)}) collective-permute-start(f32[2,4,1,512]{3,2,1,0:T(1,128)S(1)} %slice.377), channel_id=1, source_target_pairs={{4,0},{8,4},{12,8},{5,1},{9,5},{13,9},{6,2},{10,6},{14,10},{7,3},{... | collective-permute-start | bytes 49160 | tf_op jit(solution)/shard_map/ppermute | solution.py:18
  36.7 11.7 %collective-permute-start.5 = (f32[2,4,1,512]{3,2,1,0:T(1,128)S(1)}, f32[2,4,1,512]{3,2,1,0:T(1,128)S(1)}, u32[]{:S(2)}, u32[]{:S(2)}) collective-permute-start(f32[2,4,1,512]{3,2,1,0:T(1,128)S(1)} %slice.375), channel_id=1, source_target_pairs={{4,0},{8,4},{12,8},{5,1},{9,5},{13,9},{6,2},{10,6},{14,10},{7,3},{... | collective-permute-start | bytes 49160 | tf_op jit(solution)/shard_map/ppermute | solution.py:18
  38.0 10.4 %collective-permute-start.8 = (f32[2,4,1,512]{3,2,1,0:T(1,128)S(1)}, f32[2,4,1,512]{3,2,1,0:T(1,128)S(1)}, u32[]{:S(2)}, u32[]{:S(2)}) collective-permute-start(f32[2,4,1,512]{3,2,1,0:T(1,128)S(1)} %slice.380), channel_id=1, source_target_pairs={{0,4},{4,8},{8,12},{1,5},{5,9},{9,13},{2,6},{6,10},{10,14},{3,7},{... | collective-permute-start | bytes 49160 | tf_op jit(solution)/shard_map/ppermute | solution.py:18
  42.9 15.2 %collective-permute-start.16 = (bf16[4,2,8,512]{3,2,0,1:T(8,128)(2,1)S(1)}, bf16[4,2,8,512]{3,2,0,1:T(8,128)(2,1)S(1)}, u32[]{:S(2)}, u32[]{:S(2)}) collective-permute-start(bf16[4,2,8,512]{3,2,0,1:T(8,128)(2,1)S(1)} %pad_maximum_fusion.8), channel_id=1, source_target_pairs={} | collective-permute-start | bytes 196616 | tf_op jit(solution)/shard_map/ppermute | solution.py:18
  43.5 15.9 %collective-permute-start.17 = (bf16[4,2,8,512]{3,2,0,1:T(8,128)(2,1)S(1)}, bf16[4,2,8,512]{3,2,0,1:T(8,128)(2,1)S(1)}, u32[]{:S(2)}, u32[]{:S(2)}) collective-permute-start(bf16[4,2,8,512]{3,2,0,1:T(8,128)(2,1)S(1)} %pad_maximum_fusion.8), channel_id=1, source_target_pairs={{0,12},{1,13},{2,14},{3,15},{16,28},{17,29},{18,30},{19,31}} | collective-permute-start | bytes 196616 | tf_op jit(solution)/shard_map/ppermute | solution.py:18
  46.5 14.2 %collective-permute-start.18 = (bf16[4,2,8,512]{3,2,0,1:T(8,128)(2,1)S(1)}, bf16[4,2,8,512]{3,2,0,1:T(8,128)(2,1)S(1)}, u32[]{:S(2)}, u32[]{:S(2)}) collective-permute-start(bf16[4,2,8,512]{3,2,0,1:T(8,128)(2,1)S(1)} %pad_maximum_fusion.8), channel_id=1, source_target_pairs={{0,8},{4,12},{1,9},{5,13},{2,10},{6,14},{3,11},{7,15},{16,24},{20,... | collective-permute-start | bytes 196616 | tf_op jit(solution)/shard_map/ppermute | solution.py:18
  54.6 6.8 %collective-permute-start.19 = (bf16[4,2,8,512]{3,2,0,1:T(8,128)(2,1)S(1)}, bf16[4,2,8,512]{3,2,0,1:T(8,128)(2,1)S(1)}, u32[]{:S(2)}, u32[]{:S(2)}) collective-permute-start(bf16[4,2,8,512]{3,2,0,1:T(8,128)(2,1)S(1)} %pad_maximum_fusion.8), channel_id=1, source_target_pairs={{0,4},{4,8},{8,12},{1,5},{5,9},{9,13},{2,6},{6,10},{10,14},{3,7},{... | collective-permute-start | bytes 196616 | tf_op jit(solution)/shard_map/ppermute | solution.py:18
  56.6 12.4 %collective-permute-start.20 = (bf16[4,2,8,512]{3,2,0,1:T(8,128)(2,1)S(1)}, bf16[4,2,8,512]{3,2,0,1:T(8,128)(2,1)S(1)}, u32[]{:S(2)}, u32[]{:S(2)}) collective-permute-start(bf16[4,2,8,512]{3,2,0,1:T(8,128)(2,1)S(1)} %pad_maximum_fusion.8), channel_id=1, source_target_pairs={{4,0},{8,4},{12,8},{5,1},{9,5},{13,9},{6,2},{10,6},{14,10},{7,3},{... | collective-permute-start | bytes 196616 | tf_op jit(solution)/shard_map/ppermute | solution.py:18
  58.1 12.2 %collective-permute-start.21 = (bf16[4,2,8,512]{3,2,0,1:T(8,128)(2,1)S(1)}, bf16[4,2,8,512]{3,2,0,1:T(8,128)(2,1)S(1)}, u32[]{:S(2)}, u32[]{:S(2)}) collective-permute-start(bf16[4,2,8,512]{3,2,0,1:T(8,128)(2,1)S(1)} %pad_maximum_fusion.8), channel_id=1, source_target_pairs={{8,0},{12,4},{9,1},{13,5},{10,2},{14,6},{11,3},{15,7},{24,16},{28,... | collective-permute-start | bytes 196616 | tf_op jit(solution)/shard_map/ppermute | solution.py:18
  59.4 12.2 %collective-permute-start.22 = (bf16[4,2,8,512]{3,2,0,1:T(8,128)(2,1)S(1)}, bf16[4,2,8,512]{3,2,0,1:T(8,128)(2,1)S(1)}, u32[]{:S(2)}, u32[]{:S(2)}) collective-permute-start(bf16[4,2,8,512]{3,2,0,1:T(8,128)(2,1)S(1)} %pad_maximum_fusion.8), channel_id=1, source_target_pairs={{12,0},{13,1},{14,2},{15,3},{28,16},{29,17},{30,18},{31,19}} | collective-permute-start | bytes 196616 | tf_op jit(solution)/shard_map/ppermute | solution.py:18
  60.8 37.2 %collective-permute-start.23 = (bf16[4,2,8,512]{3,2,0,1:T(8,128)(2,1)S(1)}, bf16[4,2,8,512]{3,2,0,1:T(8,128)(2,1)S(1)}, u32[]{:S(2)}, u32[]{:S(2)}) collective-permute-start(bf16[4,2,8,512]{3,2,0,1:T(8,128)(2,1)S(1)} %pad_maximum_fusion.9), channel_id=1, source_target_pairs={} | collective-permute-start | bytes 196616 | tf_op jit(solution)/shard_map/ppermute | solution.py:18
  61.4 37.8 %collective-permute-start.24 = (bf16[4,2,8,512]{3,2,0,1:T(8,128)(2,1)S(1)}, bf16[4,2,8,512]{3,2,0,1:T(8,128)(2,1)S(1)}, u32[]{:S(2)}, u32[]{:S(2)}) collective-permute-start(bf16[4,2,8,512]{3,2,0,1:T(8,128)(2,1)S(1)} %pad_maximum_fusion.9), channel_id=1, source_target_pairs={{0,12},{1,13},{2,14},{3,15},{16,28},{17,29},{18,30},{19,31}} | collective-permute-start | bytes 196616 | tf_op jit(solution)/shard_map/ppermute | solution.py:18
  69.0 31.6 %collective-permute-start.25 = (bf16[4,2,8,512]{3,2,0,1:T(8,128)(2,1)S(1)}, bf16[4,2,8,512]{3,2,0,1:T(8,128)(2,1)S(1)}, u32[]{:S(2)}, u32[]{:S(2)}) collective-permute-start(bf16[4,2,8,512]{3,2,0,1:T(8,128)(2,1)S(1)} %pad_maximum_fusion.9), channel_id=1, source_target_pairs={{0,8},{4,12},{1,9},{5,13},{2,10},{6,14},{3,11},{7,15},{16,24},{20,... | collective-permute-start | bytes 196616 | tf_op jit(solution)/shard_map/ppermute | solution.py:18
  91.3 10.0 %collective-permute-start.26 = (bf16[4,2,8,512]{3,2,0,1:T(8,128)(2,1)S(1)}, bf16[4,2,8,512]{3,2,0,1:T(8,128)(2,1)S(1)}, u32[]{:S(2)}, u32[]{:S(2)}) collective-permute-start(bf16[4,2,8,512]{3,2,0,1:T(8,128)(2,1)S(1)} %pad_maximum_fusion.9), channel_id=1, source_target_pairs={{0,4},{4,8},{8,12},{1,5},{5,9},{9,13},{2,6},{6,10},{10,14},{3,7},{... | collective-permute-start | bytes 196616 | tf_op jit(solution)/shard_map/ppermute | solution.py:18
  95.8 15.9 %collective-permute-start.27 = (bf16[4,2,8,512]{3,2,0,1:T(8,128)(2,1)S(1)}, bf16[4,2,8,512]{3,2,0,1:T(8,128)(2,1)S(1)}, u32[]{:S(2)}, u32[]{:S(2)}) collective-permute-start(bf16[4,2,8,512]{3,2,0,1:T(8,128)(2,1)S(1)} %pad_maximum_fusion.9), channel_id=1, source_target_pairs={{4,0},{8,4},{12,8},{5,1},{9,5},{13,9},{6,2},{10,6},{14,10},{7,3},{... | collective-permute-start | bytes 196616 | tf_op jit(solution)/shard_map/ppermute | solution.py:18
  97.9 15.1 %collective-permute-start.28 = (bf16[4,2,8,512]{3,2,0,1:T(8,128)(2,1)S(1)}, bf16[4,2,8,512]{3,2,0,1:T(8,128)(2,1)S(1)}, u32[]{:S(2)}, u32[]{:S(2)}) collective-permute-start(bf16[4,2,8,512]{3,2,0,1:T(8,128)(2,1)S(1)} %pad_maximum_fusion.9), channel_id=1, source_target_pairs={{8,0},{12,4},{9,1},{13,5},{10,2},{14,6},{11,3},{15,7},{24,16},{28,... | collective-permute-start | bytes 196616 | tf_op jit(solution)/shard_map/ppermute | solution.py:18
  99.2 16.3 %collective-permute-start.29 = (bf16[4,2,8,512]{3,2,0,1:T(8,128)(2,1)S(1)}, bf16[4,2,8,512]{3,2,0,1:T(8,128)(2,1)S(1)}, u32[]{:S(2)}, u32[]{:S(2)}) collective-permute-start(bf16[4,2,8,512]{3,2,0,1:T(8,128)(2,1)S(1)} %pad_maximum_fusion.9), channel_id=1, source_target_pairs={{12,0},{13,1},{14,2},{15,3},{28,16},{29,17},{30,18},{31,19}} | collective-permute-start | bytes 196616 | tf_op jit(solution)/shard_map/ppermute | solution.py:18
  100.6 16.3 %collective-permute-start.30 = (bf16[4,2,8,512]{3,2,0,1:T(8,128)(2,1)S(1)}, bf16[4,2,8,512]{3,2,0,1:T(8,128)(2,1)S(1)}, u32[]{:S(2)}, u32[]{:S(2)}) collective-permute-start(bf16[4,2,8,512]{3,2,0,1:T(8,128)(2,1)S(1)} %pad_maximum_fusion.10), channel_id=1, source_target_pairs={} | collective-permute-start | bytes 196616 | tf_op jit(solution)/shard_map/ppermute | solution.py:18
  101.3 16.9 %collective-permute-start.31 = (bf16[4,2,8,512]{3,2,0,1:T(8,128)(2,1)S(1)}, bf16[4,2,8,512]{3,2,0,1:T(8,128)(2,1)S(1)}, u32[]{:S(2)}, u32[]{:S(2)}) collective-permute-start(bf16[4,2,8,512]{3,2,0,1:T(8,128)(2,1)S(1)} %pad_maximum_fusion.10), channel_id=1, source_target_pairs={{0,12},{1,13},{2,14},{3,15},{16,28},{17,29},{18,30},{19,31}} | collective-permute-start | bytes 196616 | tf_op jit(solution)/shard_map/ppermute | solution.py:18
  111.7 7.8 %collective-permute-start.32 = (bf16[4,2,8,512]{3,2,0,1:T(8,128)(2,1)S(1)}, bf16[4,2,8,512]{3,2,0,1:T(8,128)(2,1)S(1)}, u32[]{:S(2)}, u32[]{:S(2)}) collective-permute-start(bf16[4,2,8,512]{3,2,0,1:T(8,128)(2,1)S(1)} %pad_maximum_fusion.10), channel_id=1, source_target_pairs={{0,8},{4,12},{1,9},{5,13},{2,10},{6,14},{3,11},{7,15},{16,24},{20,... | collective-permute-start | bytes 196616 | tf_op jit(solution)/shard_map/ppermute | solution.py:18
  113.0 7.2 %collective-permute-start.33 = (bf16[4,2,8,512]{3,2,0,1:T(8,128)(2,1)S(1)}, bf16[4,2,8,512]{3,2,0,1:T(8,128)(2,1)S(1)}, u32[]{:S(2)}, u32[]{:S(2)}) collective-permute-start(bf16[4,2,8,512]{3,2,0,1:T(8,128)(2,1)S(1)} %pad_maximum_fusion.10), channel_id=1, source_target_pairs={{0,4},{4,8},{8,12},{1,5},{5,9},{9,13},{2,6},{6,10},{10,14},{3,7},{... | collective-permute-start | bytes 196616 | tf_op jit(solution)/shard_map/ppermute | solution.py:18
  115.5 12.3 %collective-permute-start.34 = (bf16[4,2,8,512]{3,2,0,1:T(8,128)(2,1)S(1)}, bf16[4,2,8,512]{3,2,0,1:T(8,128)(2,1)S(1)}, u32[]{:S(2)}, u32[]{:S(2)}) collective-permute-start(bf16[4,2,8,512]{3,2,0,1:T(8,128)(2,1)S(1)} %pad_maximum_fusion.10), channel_id=1, source_target_pairs={{4,0},{8,4},{12,8},{5,1},{9,5},{13,9},{6,2},{10,6},{14,10},{7,3},{... | collective-permute-start | bytes 196616 | tf_op jit(solution)/shard_map/ppermute | solution.py:18
  116.9 12.2 %collective-permute-start.35 = (bf16[4,2,8,512]{3,2,0,1:T(8,128)(2,1)S(1)}, bf16[4,2,8,512]{3,2,0,1:T(8,128)(2,1)S(1)}, u32[]{:S(2)}, u32[]{:S(2)}) collective-permute-start(bf16[4,2,8,512]{3,2,0,1:T(8,128)(2,1)S(1)} %pad_maximum_fusion.10), channel_id=1, source_target_pairs={{8,0},{12,4},{9,1},{13,5},{10,2},{14,6},{11,3},{15,7},{24,16},{28,... | collective-permute-start | bytes 196616 | tf_op jit(solution)/shard_map/ppermute | solution.py:18
  118.2 13.4 %collective-permute-start.36 = (bf16[4,2,8,512]{3,2,0,1:T(8,128)(2,1)S(1)}, bf16[4,2,8,512]{3,2,0,1:T(8,128)(2,1)S(1)}, u32[]{:S(2)}, u32[]{:S(2)}) collective-permute-start(bf16[4,2,8,512]{3,2,0,1:T(8,128)(2,1)S(1)} %pad_maximum_fusion.10), channel_id=1, source_target_pairs={{12,0},{13,1},{14,2},{15,3},{28,16},{29,17},{30,18},{31,19}} | collective-permute-start | bytes 196616 | tf_op jit(solution)/shard_map/ppermute | solution.py:18
  119.5 13.4 %collective-permute-start.37 = (bf16[4,2,8,512]{3,2,0,1:T(8,128)(2,1)S(1)}, bf16[4,2,8,512]{3,2,0,1:T(8,128)(2,1)S(1)}, u32[]{:S(2)}, u32[]{:S(2)}) collective-permute-start(bf16[4,2,8,512]{3,2,0,1:T(8,128)(2,1)S(1)} %pad_maximum_fusion.11), channel_id=1, source_target_pairs={} | collective-permute-start | bytes 196616 | tf_op jit(solution)/shard_map/ppermute | solution.py:18
  120.2 14.1 %collective-permute-start.38 = (bf16[4,2,8,512]{3,2,0,1:T(8,128)(2,1)S(1)}, bf16[4,2,8,512]{3,2,0,1:T(8,128)(2,1)S(1)}, u32[]{:S(2)}, u32[]{:S(2)}) collective-permute-start(bf16[4,2,8,512]{3,2,0,1:T(8,128)(2,1)S(1)} %pad_maximum_fusion.11), channel_id=1, source_target_pairs={{0,12},{1,13},{2,14},{3,15},{16,28},{17,29},{18,30},{19,31}} | collective-permute-start | bytes 196616 | tf_op jit(solution)/shard_map/ppermute | solution.py:18
  127.8 8.0 %collective-permute-start.39 = (bf16[4,2,8,512]{3,2,0,1:T(8,128)(2,1)S(1)}, bf16[4,2,8,512]{3,2,0,1:T(8,128)(2,1)S(1)}, u32[]{:S(2)}, u32[]{:S(2)}) collective-permute-start(bf16[4,2,8,512]{3,2,0,1:T(8,128)(2,1)S(1)} %pad_maximum_fusion.11), channel_id=1, source_target_pairs={{0,8},{4,12},{1,9},{5,13},{2,10},{6,14},{3,11},{7,15},{16,24},{20,... | collective-permute-start | bytes 196616 | tf_op jit(solution)/shard_map/ppermute | solution.py:18
  133.0 7.1 %collective-permute-start.42 = (bf16[4,2,8,512]{3,2,0,1:T(8,128)(2,1)S(1)}, bf16[4,2,8,512]{3,2,0,1:T(8,128)(2,1)S(1)}, u32[]{:S(2)}, u32[]{:S(2)}) collective-permute-start(bf16[4,2,8,512]{3,2,0,1:T(8,128)(2,1)S(1)} %pad_maximum_fusion.11), channel_id=1, source_target_pairs={{8,0},{12,4},{9,1},{13,5},{10,2},{14,6},{11,3},{15,7},{24,16},{28,... | collective-permute-start | bytes 196616 | tf_op jit(solution)/shard_map/ppermute | solution.py:18
  134.3 9.1 %collective-permute-start.43 = (bf16[4,2,8,512]{3,2,0,1:T(8,128)(2,1)S(1)}, bf16[4,2,8,512]{3,2,0,1:T(8,128)(2,1)S(1)}, u32[]{:S(2)}, u32[]{:S(2)}) collective-permute-start(bf16[4,2,8,512]{3,2,0,1:T(8,128)(2,1)S(1)} %pad_maximum_fusion.11), channel_id=1, source_target_pairs={{12,0},{13,1},{14,2},{15,3},{28,16},{29,17},{30,18},{31,19}} | collective-permute-start | bytes 196616 | tf_op jit(solution)/shard_map/ppermute | solution.py:18
  (22 other events, 191.0 us)
Sparse Core Ops, SparseCore 0:
  164.7 29.6 reduce-scatter.1
where the time goes:
time: 206 us; the launch traced here: 205 us
  starting transfers between devices  107 us (52%)
  waiting for transfers between devices  42.2 us (20%)
  local copies, waits for them, and re-layouts  19.5 us (9%)
  between operations  15.5 us (8%)
  matrix products  12.7 us (6%)
  other arithmetic  7.86 us (4%)
    ppermute x44, starting transfers between devices, passed_along(): lax.ppermute(value, axis, [(source, source + steps) for source in range(i...  107 us
    reduce_scatter x1, waiting for transfers between devices, shards(): lax.psum_scatter(jnp.einsum('hxy,cxyz->hcxz', select, correlated, precisi...  27.4 us
    ppermute x44, waiting for transfers between devices, passed_along(): lax.ppermute(value, axis, [(source, source + steps) for source in range(i...  14.8 us
    dot_general x1, matrix products, shards(): jnp.einsum('tsxz,tscyz->cxyz', source_all, window_all, preferred_element_...  7.98 us
    another operation x1, local copies, waits for them, and re-layouts, shards(): window_all = jnp.stack(window_list)  5.54 us
    unnamed x59, local copies, waits for them, and re-layouts  5.22 us
  transfers between devices with their start and end apart: 45, of which 9 were waited for; matrix products, arithmetic and copies ran while one was open for 6% of the time, Pallas kernels for 0%

commit v1 on v0

v1 whole, which is shorter than its diff:
```python
import functools
import math

import jax
import jax.numpy as jnp
from jax import lax
from jax.experimental import pallas as pl
from jax.experimental.pallas import tpu as pltpu
from jax.sharding import PartitionSpec as P

STEPS = 4
SHIFT = 32
LANES = 128
DT = 0.3
F32 = jnp.float32
BF16 = jnp.bfloat16
MESH = pl.DeviceIdType.MESH


def kernel(
    n_slab, n_shot, reach, shots, noff,
    src_ref, rec_ref, vp_ref, vs_ref, rho_ref, data_ref, sx_ref, sz_ref, rx_ref, rz_ref, off_ref,
    fs_ref, fr_ref, ovp_ref, ovs_ref, orho_ref,
    model, inj, spread, rho_l, rho_r, to_r, to_l, from_l, from_r, edge, srcf, win, wf,
    part, part_bf, r1, s2, r2,
    halo_send, halo_recv, rho_send, rho_recv, win_send, win_recv, r1_send, r1_recv, r2_send, r2_recv,
):
    width, depth = rho_ref.shape
    zc_n = depth // LANES
    per = noff // n_shot
    na = n_shot // 2
    span = SHIFT // width
    me = lax.axis_index("slab")
    shot = lax.axis_index("shot")
    par = lax.rem(shot, 2)
    mate = shot + 1 - 2 * par
    mine = shot // 2
    has_l = me > 0
    has_r = me < n_slab - 1

    barrier = pltpu.get_barrier_semaphore()

    def greet(axis, index):
        pl.semaphore_signal(barrier, inc=1, device_id={axis: index}, device_id_type=MESH)

    for k in range(1, reach + 1):
        pl.when(me - k >= 0)(functools.partial(greet, "slab", me - k))
        pl.when(me + k < n_slab)(functools.partial(greet, "slab", me + k))
    greet("shot", mate)
    for q in range(1, na):
        greet("shot", 2 * lax.rem(mine + q, na) + par)

    row = lax.broadcasted_iota(jnp.int32, (width, depth), 0)
    lane = lax.broadcasted_iota(jnp.int32, (width, depth), 1)

    def back_z(f):
        return f - jnp.where(lane == 0, 0.0, pltpu.roll(f, 1, 1))

    def fore_z(f):
        return jnp.where(lane == depth - 1, 0.0, pltpu.roll(f, depth - 1, 1)) - f

    def down(f, halo):
        return jnp.where(row == 0, halo, pltpu.roll(f, 1, 0))

    def up(f, halo):
        return jnp.where(row == width - 1, halo, pltpu.roll(f, width - 1, 0))

    def pack(t, ws, fields):
        vx, vz, sxx, szz, sxz = fields
        one = pl.ds(ws, 1)
        for slot, f in enumerate((sxx, szz, sxz, vz)):
            to_r[t, slot, one, :] = f[width - 1 : width, :]
        for slot, f in enumerate((vx, sxx, sxz)):
            to_l[t, slot, one, :] = f[0:1, :]

    for w, ref in enumerate((src_ref, rec_ref)):

        def first(s, carry, w=w, ref=ref):
            pack(0, w * shots + s, [ref[s, i] for i in range(5)])
            return carry

        lax.fori_loop(0, shots, first, 0)

    count = sum(
        (me - k >= 0).astype(jnp.int32) + (me + k < n_slab).astype(jnp.int32)
        for k in range(1, reach + 1)
    ) + na
    pl.semaphore_wait(barrier, count)

    def halo_copy(t, right):
        if right:
            return pltpu.make_async_remote_copy(
                src_ref=to_r.at[t], dst_ref=from_l.at[t],
                send_sem=halo_send.at[t, 0], recv_sem=halo_recv.at[t, 0],
                device_id={"slab": me + 1}, device_id_type=MESH)
        return pltpu.make_async_remote_copy(
            src_ref=to_l.at[t], dst_ref=from_r.at[t],
            send_sem=halo_send.at[t, 1], recv_sem=halo_recv.at[t, 1],
            device_id={"slab": me - 1}, device_id_type=MESH)

    def rho_copy(right):
        if right:
            return pltpu.make_async_remote_copy(
                src_ref=rho_ref, dst_ref=rho_l, send_sem=rho_send.at[0], recv_sem=rho_recv.at[0],
                device_id={"slab": me + 1}, device_id_type=MESH)
        return pltpu.make_async_remote_copy(
            src_ref=rho_ref, dst_ref=rho_r, send_sem=rho_send.at[1], recv_sem=rho_recv.at[1],
            device_id={"slab": me - 1}, device_id_type=MESH)

    def send_halo(t):
        pl.when(has_r)(lambda: halo_copy(t, True).start())
        pl.when(has_l)(lambda: halo_copy(t, False).start())

    send_halo(0)
    pl.when(has_r)(lambda: rho_copy(True).start())
    pl.when(has_l)(lambda: rho_copy(False).start())

    def win_copy(t, from_slot, to_slot, target):
        return pltpu.make_async_remote_copy(
            src_ref=win.at[t, from_slot], dst_ref=win.at[t, to_slot],
            send_sem=win_send.at[t, to_slot], recv_sem=win_recv.at[t, to_slot],
            device_id={"slab": target}, device_id_type=MESH)

    def hop(t, k):
        right = win_copy(t, reach - k + 1, reach - k, me + 1)
        left = win_copy(t, reach + k - 1, reach + k, me - 1)
        pl.when(has_r & (me - k + 1 >= 0))(lambda: right.start())
        pl.when(has_l & (me + k - 1 < n_slab))(lambda: left.start())

    def hop_wait(t, k):
        pl.when(me - k >= 0)(lambda: win_copy(t, reach - k + 1, reach - k, me + 1).wait_recv())
        pl.when(me + k < n_slab)(lambda: win_copy(t, reach + k - 1, reach + k, me - 1).wait_recv())

    def hop_done(t, k):
        pl.when(has_r & (me - k + 1 >= 0))(
            lambda: win_copy(t, reach - k + 1, reach - k, me + 1).wait_send())
        pl.when(has_l & (me + k - 1 < n_slab))(
            lambda: win_copy(t, reach + k - 1, reach + k, me - 1).wait_send())

    rho = rho_ref[...]
    vp = vp_ref[...]
    vs = vs_ref[...]
    shear = rho * vs * vs
    lame = rho * (vp * vp - 2.0 * vs * vs)
    model[0] = 1.0 / rho
    model[1] = shear
    model[2] = lame
    model[3] = lame + 2.0 * shear

    @pl.when(jnp.logical_not(has_l))
    def _():
        from_l[...] = jnp.zeros_like(from_l)
        rho_l[...] = jnp.ones_like(rho_l)

    @pl.when(jnp.logical_not(has_r))
    def _():
        from_r[...] = jnp.zeros_like(from_r)
        rho_r[...] = jnp.ones_like(rho_r)

    nrec = data_ref.shape[2]
    rel = rx_ref[...] - me * width
    at_x = rel == lax.broadcasted_iota(jnp.int32, (width, nrec), 0)
    for s in range(shots):
        for t in range(STEPS):
            spread[pl.ds((t * shots + s) * width, width), :] = jnp.where(
                at_x, data_ref[s, t : t + 1, :], 0.0)
    at_z = jnp.where(
        lax.broadcasted_iota(jnp.int32, (depth, nrec), 0) == rz_ref[...], 1.0, 0.0).astype(BF16)
    rest = spread[...]
    total = None
    for _ in range(3):
        piece = rest.astype(BF16)
        rest = rest - piece.astype(F32)
        term = lax.dot_general(piece, at_z, (((1,), (1,)), ((), ())), preferred_element_type=F32)
        total = term if total is None else total + term
    inj[...] = total

    def zero(i, carry):
        wf[0, i] = jnp.zeros(wf.shape[2:], F32)
        wf[1, i] = jnp.zeros(wf.shape[2:], F32)
        return carry

    lax.fori_loop(0, STEPS * shots, zero, 0)

    sign_rows = jnp.where(row < shots, DT, -DT)

    def widen(t, slot):
        base = (slot - reach + span) * width

        def body(s, carry):
            both = win[t, slot, s].astype(F32)
            for zc in range(zc_n):
                cut = both[:, zc * LANES : (zc + 1) * LANES]
                wf[0, t * shots + s, zc, base : base + width, :] = cut[:width]
                wf[1, t * shots + s, zc, base : base + width, :] = cut[width:]
            return carry

        lax.fori_loop(0, shots, body, 0)

    for t in range(STEPS):
        pl.when(has_l)(lambda: halo_copy(t, True).wait_recv())
        pl.when(has_r)(lambda: halo_copy(t, False).wait_recv())
        if t == 0:
            pl.when(has_l)(lambda: rho_copy(True).wait_recv())
            pl.when(has_r)(lambda: rho_copy(False).wait_recv())
        buoy_l = jnp.where(has_l, 1.0 / rho_l[width - 1 : width, :], 0.0)
        buoy_r = jnp.where(has_r, 1.0 / rho_r[0:1, :], 0.0)
        edge[0] = from_l[t, 3] + sign_rows * buoy_l * (
            to_l[t, 2] - from_l[t, 2] + fore_z(from_l[t, 1]))
        edge[1] = from_r[t, 0] + sign_rows * buoy_r * (
            from_r[t, 1] - to_r[t, 0] + back_z(from_r[t, 2]))
        wavelet = 2.0 * math.cos(1.3 * t + 0.4)
        for w in range(2):
            state = (fs_ref, fr_ref)[w]
            before = ((src_ref, rec_ref)[w]) if t == 0 else state
            sg = (DT, -DT)[w]

            def step(s, carry, w=w, state=state, before=before, sg=sg, t=t, wavelet=wavelet):
                ws = w * shots + s
                one = pl.ds(ws, 1)
                vx, vz, sxx, szz, sxz = [before[s, i] for i in range(5)]
                buoy = sg * model[0]
                vx = vx + buoy * (sxx - down(sxx, from_l[t, 0, one, :]) + back_z(sxz))
                vz = vz + buoy * (up(sxz, from_r[t, 2, one, :]) - sxz + fore_z(szz))
                stretch = sg * (up(vx, edge[1, one, :]) - vx)
                squeeze = sg * back_z(vz)
                slide_x = vz - down(vz, edge[0, one, :])
                slide_z = fore_z(vx)
                if w == 0:
                    here = (row + me * width == sx_ref[s]) & (lane == sz_ref[s])
                    add = jnp.where(here, wavelet, 0.0)
                else:
                    start = pl.multiple_of((t * shots + s) * width, width)
                    add = inj[pl.ds(start, width), :]
                sxx = sxx + (model[3] * stretch + model[2] * squeeze) + add
                szz = szz + (model[2] * stretch + model[3] * squeeze) + add
                sxz = sxz + sg * model[1] * (slide_x + slide_z)
                for i, f in enumerate((vx, vz, sxx, szz, sxz)):
                    state[s, i] = f
                if t < STEPS - 1:
                    pack(t + 1, ws, (vx, vz, sxx, szz, sxz))
                pressure = -0.5 * (sxx + szz)
                if w == 0:
                    rounded = pressure.astype(BF16).astype(F32)
                    for zc in range(zc_n):
                        srcf[t * shots + s, zc] = rounded[:, zc * LANES : (zc + 1) * LANES]
                else:
                    win[t, reach, s] = jnp.concatenate([pressure, slide_z - slide_x], 0).astype(BF16)
                return carry

            lax.fori_loop(0, shots, step, 0)
        if t < STEPS - 1:
            send_halo(t + 1)
        hop(t, 1)
        for k in range(2, reach + 1):
            if t - k + 1 >= 0:
                hop_wait(t - k + 1, k - 1)
                hop(t - k + 1, k)
        widen(t, reach)

    for late in range(1, reach + 1):
        for k in range(2, reach + 1):
            t = STEPS - 1 + late - k + 1
            if 0 <= t < STEPS:
                hop_wait(t, k - 1)
                hop(t, k)
    for t in range(STEPS):
        hop_wait(t, reach)
        for k in range(1, reach + 1):
            pl.when(me - k >= 0)(functools.partial(widen, t, reach - k))
            pl.when(me + k < n_slab)(functools.partial(widen, t, reach + k))

    scale = 1.0 / (shots * n_shot * STEPS)

    def correlate(owner):
        h0 = pl.multiple_of(owner * per, 8)

        def over_z(zc, carry):
            def over_ts(ts, sums):
                source = srcf[ts, zc]
                out = []
                for c in range(2):
                    for p in range(per + 1):
                        out.append(
                            sums[c * (per + 1) + p]
                            + source * wf[c, ts, zc, pl.ds(h0 + p, width), :])
                return tuple(out)

            sums = lax.fori_loop(
                0, STEPS * shots, over_ts,
                tuple(jnp.zeros((width, LANES), F32) for _ in range(2 * (per + 1))), unroll=2)
            at = pl.ds(pl.multiple_of(zc * LANES, LANES), LANES)
            for p in range(per):
                keep = off_ref[h0 + p] == h0 + p - SHIFT
                both = scale * jnp.concatenate(
                    [jnp.where(keep, sums[c * (per + 1) + p], sums[c * (per + 1) + p + 1])
                     for c in range(2)], 0)
                part[h0 + p, :, at] = both
                part_bf[h0 + p, :, at] = both.astype(BF16)
            return carry

        lax.fori_loop(0, zc_n, over_z, 0)

    def r1_copy(a):
        start = (2 * a + 1 - par) * per
        return pltpu.make_async_remote_copy(
            src_ref=part_bf.at[pl.ds(start, per)], dst_ref=r1.at[a],
            send_sem=r1_send.at[a], recv_sem=r1_recv.at[a],
            device_id={"shot": mate}, device_id_type=MESH)

    for q in range(1, na + 1):
        a = lax.rem(mine + q, na)
        correlate(2 * a + 1 - par)
        r1_copy(a).start()

    def r2_copy(q):
        a = lax.rem(mine + q, na)
        return pltpu.make_async_remote_copy(
            src_ref=s2.at[q - 1], dst_ref=r2.at[q - 1],
            send_sem=r2_send.at[q - 1], recv_sem=r2_recv.at[q - 1],
            device_id={"shot": 2 * a + par}, device_id_type=MESH)

    for q in range(1, na):
        a = lax.rem(mine + q, na)
        owner = 2 * a + par
        correlate(owner)
        r1_copy(a).wait_recv()

        def join(p, carry, a=a, owner=owner, q=q):
            s2[q - 1, p] = (part[owner * per + p] + r1[a, p].astype(F32)).astype(BF16)
            return carry

        lax.fori_loop(0, per, join, 0)
        r2_copy(q).start()
    correlate(shot)
    r1_copy(mine).wait_recv()
    for q in range(1, na):
        r2_copy(q).wait_recv()

    ratio = vs / vp
    coef = 2.0 * ratio * ratio
    rho_vp = 2.0 * rho * vp
    rho_vs = 2.0 * rho * vs

    def finish(p, carry):
        both = part[shot * per + p] + r1[mine, p].astype(F32)
        for q in range(1, na):
            both = both + r2[q - 1, p].astype(F32)
        pp = both[:width]
        ps = both[width:]
        ovp_ref[p] = rho_vp * pp
        ovs_ref[p] = rho_vs * (ps - coef * pp)
        orho_ref[p] = vp * vp * pp + vs * vs * ps
        return carry

    lax.fori_loop(0, per, finish, 0)

    for t in range(STEPS):
        pl.when(has_r)(lambda: halo_copy(t, True).wait_send())
        pl.when(has_l)(lambda: halo_copy(t, False).wait_send())
        for k in range(1, reach + 1):
            hop_done(t, k)
    pl.when(has_r)(lambda: rho_copy(True).wait_send())
    pl.when(has_l)(lambda: rho_copy(False).wait_send())
    for a in range(na):
        r1_copy(lax.rem(mine + a, na)).wait_send()
    for q in range(1, na):
        r2_copy(q).wait_send()


def shards(n_slab, n_shot, source_state, receiver_state, p_velocity, s_velocity, density,
           receiver_data, source_x, source_z, receiver_x, receiver_z, offsets):
    shots, _, width, depth = source_state.shape
    noff = offsets.shape[0]
    nrec = receiver_x.shape[0]
    span = SHIFT // width
    reach = min(span, n_slab - 1)
    per = noff // n_shot
    na = n_shot // 2
    rows = 2 * shots
    slots = 2 * reach + 1
    nz = depth // LANES
    ts = STEPS * shots
    vmem = pl.BlockSpec(memory_space=pltpu.VMEM)
    smem = pl.BlockSpec(memory_space=pltpu.SMEM)
    image = jax.ShapeDtypeStruct((per, width, depth), F32)
    state = jax.ShapeDtypeStruct(source_state.shape, F32)
    dma = pltpu.SemaphoreType.DMA
    return pl.pallas_call(
        functools.partial(kernel, n_slab, n_shot, reach, shots, noff),
        out_shape=(state, state, image, image, image),
        in_specs=[vmem] * 6 + [smem, smem, vmem, vmem, smem],
        out_specs=(vmem,) * 5,
        scratch_shapes=[
            pltpu.VMEM((4, width, depth), F32),
            pltpu.VMEM((ts * width, depth), F32),
            pltpu.VMEM((ts * width, nrec), F32),
            pltpu.VMEM((width, depth), F32),
            pltpu.VMEM((width, depth), F32),
            pltpu.VMEM((STEPS, 4, rows, depth), F32),
            pltpu.VMEM((STEPS, 3, rows, depth), F32),
            pltpu.VMEM((STEPS, 4, rows, depth), F32),
            pltpu.VMEM((STEPS, 3, rows, depth), F32),
            pltpu.VMEM((2, rows, depth), F32),
            pltpu.VMEM((ts, nz, width, LANES), F32),
            pltpu.VMEM((STEPS, slots, shots, 2 * width, depth), BF16),
            pltpu.VMEM((2, ts, nz, (2 * span + 1) * width, LANES), F32),
            pltpu.VMEM((noff, 2 * width, depth), F32),
            pltpu.VMEM((noff, 2 * width, depth), BF16),
            pltpu.VMEM((na, per, 2 * width, depth), BF16),
            pltpu.VMEM((na - 1, per, 2 * width, depth), BF16),
            pltpu.VMEM((na - 1, per, 2 * width, depth), BF16),
            dma((STEPS, 2)), dma((STEPS, 2)), dma((2,)), dma((2,)),
            dma((STEPS, slots)), dma((STEPS, slots)),
            dma((na,)), dma((na,)), dma((na - 1,)), dma((na - 1,)),
        ],
        compiler_params=pltpu.CompilerParams(
            collective_id=0, has_side_effects=True, vmem_limit_bytes=40 * 2**20),
    )(source_state, receiver_state, p_velocity, s_velocity, density, receiver_data,
      source_x, source_z, receiver_x.reshape(1, nrec), receiver_z.reshape(1, nrec), offsets)


def solution(mesh):
    return jax.shard_map(
        functools.partial(shards, mesh.shape["slab"], mesh.shape["shot"]),
        mesh=mesh,
        in_specs=(
            P(("group", "shot"), None, "slab", None),
            P(("group", "shot"), None, "slab", None),
            P(("group", "slab"), None),
            P(("group", "slab"), None),
            P(("group", "slab"), None),
            P(("group", "shot"), None, None),
            P(("group", "shot")),
            P(("group", "shot")),
            P("group"),
            P("group"),
            P(),
        ),
        out_specs=(
            P(("group", "shot"), None, "slab", None),
            P(("group", "shot"), None, "slab", None),
            P(("group", "shot"), "slab", None),
            P(("group", "shot"), "slab", None),
            P(("group", "shot"), "slab", None),
        ),
        check_vma=False,
    )
```

time: 206 us -> 56.6 us (0.27)
  starting transfers between devices: 107 us -> 0 us
  Pallas kernels: 0 us -> 46.3 us
  waiting for transfers between devices: 42.2 us -> 0 us
  between operations: 15.5 us -> 0.69 us
  matrix products: 12.7 us -> 0 us
  local copies, waits for them, and re-layouts: 19.5 us -> 9.06 us
  other arithmetic: 7.86 us -> 0 us
    ppermute x44 -> x0, starting transfers between devices: 107 us -> none  [passed_along(): lax.ppermute(value, axis, [(source, source + steps) for source in range(i...]
    pallas_call x0 -> x1, Pallas kernels: none -> 46.3 us  [shards(): pl.pallas_call(functools.partial(kernel, n_slab, n_shot, reach, shots, no...]
    reduce_scatter x1 -> x0, waiting for transfers between devices: 27.4 us -> none  [shards(): lax.psum_scatter(jnp.einsum('hxy,cxyz->hcxz', select, correlated, precisi...]
    ppermute x44 -> x0, waiting for transfers between devices: 14.8 us -> none  [passed_along(): lax.ppermute(value, axis, [(source, source + steps) for source in range(i...]
    dot_general x6 -> x0, matrix products: 12.7 us -> none  [the longest x1 7.98 us: shards(): jnp.einsum('tsxz,tscyz->cxyz', source_all, window_all, preferred_element_...]
    another operation x4 -> x0, local copies, waits for them, and re-layouts: 9.55 us -> none  [the longest x1 5.54 us: shards(): window_all = jnp.stack(window_list)]
    unnamed x59 -> x27, local copies, waits for them, and re-layouts: 5.22 us -> 9.06 us
    dot_general x1 -> x0, local copies, waits for them, and re-layouts: 3.55 us -> none  [shards(): jnp.einsum('tsxz,tscyz->cxyz', source_all, window_all, preferred_element_...]
  transfers between devices with their start and end apart: 45 -> 0, of which waited for: 9 -> 0; matrix products, arithmetic and copies ran while one was open for 6% -> 0% of each run, Pallas kernels for 0% -> 0%
where the time goes in v1:
time: 56.6 us; the launch traced here: 56 us
  Pallas kernels  46.3 us (82%)
  local copies, waits for them, and re-layouts  9.06 us (16%)
  between operations  0.69 us (1%)
    pallas_call x1, Pallas kernels, shards(): pl.pallas_call(functools.partial(kernel, n_slab, n_shot, reach, shots, no...  46.3 us
    unnamed x27, local copies, waits for them, and re-layouts  9.06 us

profile of v1, /device:TPU:0, one launch (start us, length us, event | category | flops | bytes accessed | tf_op | source)
XLA Modules:
  0.0 56.0 jit_solution(3437830959226257959)
XLA Ops:
  0.6 0.0 copy-start.7
  0.6 0.0 copy-start.9
  0.7 0.0 copy-start.10
  0.7 0.0 copy-start.6
  0.7 0.0 copy-start.8
  0.7 0.6 %copy-done.7 = s32[256]{0:T(256)S(1)} copy-done((s32[256]{0:T(256)S(1)}, s32[256]{0:T(256)}, u32[]{:S(2)}) %copy-start.7) | copy-done | bytes 1048
  1.3 0.0 copy-done.9
  1.3 0.0 copy-done.10
  1.3 0.0 copy-done.6
  1.4 0.0 copy-done.8
  1.4 0.0 copy-start
  1.4 1.0 %copy-done = f32[4,5,8,512]{3,2,1,0:T(8,128)S(1)} copy-done((f32[4,5,8,512]{3,2,1,0:T(8,128)S(1)}, f32[4,5,8,512]{3,2,1,0:T(8,128)}, u32[]{:S(2)}) %copy-start) | copy-done | bytes 327704
  2.3 0.0 copy-start.1
  2.3 1.0 %copy-done.1 = f32[4,5,8,512]{3,2,1,0:T(8,128)S(1)} copy-done((f32[4,5,8,512]{3,2,1,0:T(8,128)S(1)}, f32[4,5,8,512]{3,2,1,0:T(8,128)}, u32[]{:S(2)}) %copy-start.1) | copy-done | bytes 327704
  3.3 0.0 copy-start.2
  3.3 0.7 %copy-done.2 = f32[8,512]{1,0:T(8,128)S(1)} copy-done((f32[8,512]{1,0:T(8,128)S(1)}, f32[8,512]{1,0:T(8,128)}, u32[]{:S(2)}) %copy-start.2) | copy-done | bytes 16408
  4.0 0.0 copy-start.3
  4.0 0.7 %copy-done.3 = f32[8,512]{1,0:T(8,128)S(1)} copy-done((f32[8,512]{1,0:T(8,128)S(1)}, f32[8,512]{1,0:T(8,128)}, u32[]{:S(2)}) %copy-start.3) | copy-done | bytes 16408
  4.7 0.0 copy-start.4
  4.8 0.7 %copy-done.4 = f32[8,512]{1,0:T(8,128)S(1)} copy-done((f32[8,512]{1,0:T(8,128)S(1)}, f32[8,512]{1,0:T(8,128)}, u32[]{:S(2)}) %copy-start.4) | copy-done | bytes 16408
  5.5 0.0 copy-start.5
  5.5 0.7 %copy-done.5 = f32[4,4,256]{2,1,0:T(4,128)S(1)} copy-done((f32[4,4,256]{2,1,0:T(4,128)S(1)}, f32[4,4,256]{2,1,0:T(4,128)}, u32[]{:S(2)}) %copy-start.5) | copy-done | bytes 16408
  6.2 46.3 %shard_map.146 = (f32[4,5,8,512]{3,2,1,0:T(8,128)S(1)}, f32[4,5,8,512]{3,2,1,0:T(8,128)S(1)}, f32[16,8,512]{2,1,0:T(8,128)S(1)}, f32[16,8,512]{2,1,0:T(8,128)S(1)}, f32[16,8,512]{2,1,0:T(8,128)S(1)}) custom-call(f32[4,5,8,512]{3,2,1,0:T(8,128)S(1)} %copy-done, f32[4,5,8,512]{3,2,1,0:T(8,128)S(1)} %copy-done.1, f32[8,512]{1,0:T(8,128)S(1)} %copy-done.2, ...), custom_call_target="tpu_custom_call" | custom-call | tf_op jit(solution)/shard_map/pallas_call | solution.py:389
  52.5 0.7 %copy.21 = f32[4,5,8,512]{3,2,1,0:T(8,128)} copy(f32[4,5,8,512]{3,2,1,0:T(8,128)S(1)} %get-tuple-element.10) | data formatting | bytes 655360
  53.2 0.7 %copy.22 = f32[4,5,8,512]{3,2,1,0:T(8,128)} copy(f32[4,5,8,512]{3,2,1,0:T(8,128)S(1)} %get-tuple-element.11) | data formatting | bytes 655360
  53.9 0.7 %copy.23 = f32[16,8,512]{2,1,0:T(8,128)} copy(f32[16,8,512]{2,1,0:T(8,128)S(1)} %get-tuple-element.12) | data formatting | bytes 524288
  54.6 0.7 %copy.24 = f32[16,8,512]{2,1,0:T(8,128)} copy(f32[16,8,512]{2,1,0:T(8,128)S(1)} %get-tuple-element.13) | data formatting | bytes 524288
  55.3 0.7 %copy.25 = f32[16,8,512]{2,1,0:T(8,128)} copy(f32[16,8,512]{2,1,0:T(8,128)S(1)} %get-tuple-element.14) | data formatting | bytes 524288
Async XLA Ops:
  0.6 0.7 %copy-start.7 = (s32[256]{0:T(256)S(1)}, s32[256]{0:T(256)}, u32[]{:S(2)}) copy-start(s32[256]{0:T(256)} %param.20) | copy-start | bytes 3076
  0.6 0.7 %copy-start.9 = (s32[4]{0:T(128)S(1)}, s32[4]{0:T(128)}, u32[]{:S(2)}) copy-start(s32[4]{0:T(128)} %sz_ref.1) | copy-start | bytes 52
  0.7 0.7 %copy-start.10 = (s32[64]{0:T(128)S(1)}, s32[64]{0:T(128)}, u32[]{:S(2)}) copy-start(s32[64]{0:T(128)} %off_ref.1) | copy-start | bytes 772
  0.7 0.7 %copy-start.6 = (s32[256]{0:T(256)S(1)}, s32[256]{0:T(256)}, u32[]{:S(2)}) copy-start(s32[256]{0:T(256)} %param.19) | copy-start | bytes 3076
  0.7 0.7 %copy-start.8 = (s32[4]{0:T(128)S(1)}, s32[4]{0:T(128)}, u32[]{:S(2)}) copy-start(s32[4]{0:T(128)} %sx_ref.1) | copy-start | bytes 52
  1.4 1.0 %copy-start = (f32[4,5,8,512]{3,2,1,0:T(8,128)S(1)}, f32[4,5,8,512]{3,2,1,0:T(8,128)}, u32[]{:S(2)}) copy-start(f32[4,5,8,512]{3,2,1,0:T(8,128)} %src_ref.1) | copy-start | bytes 983044
  2.3 1.0 %copy-start.1 = (f32[4,5,8,512]{3,2,1,0:T(8,128)S(1)}, f32[4,5,8,512]{3,2,1,0:T(8,128)}, u32[]{:S(2)}) copy-start(f32[4,5,8,512]{3,2,1,0:T(8,128)} %rec_ref.1) | copy-start | bytes 983044
  3.3 0.7 %copy-start.2 = (f32[8,512]{1,0:T(8,128)S(1)}, f32[8,512]{1,0:T(8,128)}, u32[]{:S(2)}) copy-start(f32[8,512]{1,0:T(8,128)} %vp_ref.1) | copy-start | bytes 49156
  4.0 0.7 %copy-start.3 = (f32[8,512]{1,0:T(8,128)S(1)}, f32[8,512]{1,0:T(8,128)}, u32[]{:S(2)}) copy-start(f32[8,512]{1,0:T(8,128)} %vs_ref.1) | copy-start | bytes 49156
  4.7 0.7 %copy-start.4 = (f32[8,512]{1,0:T(8,128)S(1)}, f32[8,512]{1,0:T(8,128)}, u32[]{:S(2)}) copy-start(f32[8,512]{1,0:T(8,128)} %rho_ref.1) | copy-start | bytes 49156
  5.5 0.7 %copy-start.5 = (f32[4,4,256]{2,1,0:T(4,128)S(1)}, f32[4,4,256]{2,1,0:T(4,128)}, u32[]{:S(2)}) copy-start(f32[4,4,256]{2,1,0:T(4,128)} %data_ref.1) | copy-start | bytes 49156

commit v2 on v1

--- a/solution.py
+++ b/solution.py
@@ -12,6 +12,7 @@
 SHIFT = 32
 LANES = 128
 DT = 0.3
+DIRECT = ()
 F32 = jnp.float32
 BF16 = jnp.bfloat16
 MESH = pl.DeviceIdType.MESH
@@ -19,8 +20,9 @@
 
 def kernel(
     n_slab, n_shot, reach, shots, noff,
-    src_ref, rec_ref, vp_ref, vs_ref, rho_ref, data_ref, sx_ref, sz_ref, rx_ref, rz_ref, off_ref,
+    src_in, rec_in, vp_in, vs_in, rho_in, data_in, sx_ref, sz_ref, rx_in, rz_in, off_ref,
     fs_ref, fr_ref, ovp_ref, ovs_ref, orho_ref,
+    src_ref, rec_ref, vp_ref, vs_ref, rho_ref, data_ref, rx_ref, rz_ref, in_sem,
     model, inj, spread, rho_l, rho_r, to_r, to_l, from_l, from_r, edge, srcf, win, wf,
     part, part_bf, r1, s2, r2,
     halo_send, halo_recv, rho_send, rho_recv, win_send, win_recv, r1_send, r1_recv, r2_send, r2_recv,
@@ -38,6 +40,15 @@
     has_l = me > 0
     has_r = me < n_slab - 1
 
+    inward = [
+        pltpu.make_async_copy(a, b, in_sem.at[i])
+        for i, (a, b) in enumerate((
+            (src_in, src_ref), (rec_in, rec_ref), (rho_in, rho_ref), (vp_in, vp_ref), (vs_in, vs_ref),
+            (data_in, data_ref), (rx_in, rx_ref), (rz_in, rz_ref)))
+    ]
+    for copy in inward:
+        copy.start()
+
     barrier = pltpu.get_barrier_semaphore()
 
     def greet(axis, index):
@@ -73,13 +84,15 @@
         for slot, f in enumerate((vx, sxx, sxz)):
             to_l[t, slot, one, :] = f[0:1, :]
 
+    for copy in inward:
+        copy.wait()
     for w, ref in enumerate((src_ref, rec_ref)):
 
         def first(s, carry, w=w, ref=ref):
             pack(0, w * shots + s, [ref[s, i] for i in range(5)])
             return carry
 
-        lax.fori_loop(0, shots, first, 0)
+        lax.fori_loop(0, shots, first, 0, unroll=True)
 
     count = sum(
         (me - k >= 0).astype(jnp.int32) + (me + k < n_slab).astype(jnp.int32)
@@ -121,21 +134,34 @@
             send_sem=win_send.at[t, to_slot], recv_sem=win_recv.at[t, to_slot],
             device_id={"slab": target}, device_id_type=MESH)
 
+    def sides(t, k):
+        if t in DIRECT:
+            return (
+                (me + k < n_slab, me - k >= 0, win_copy(t, reach, reach - k, me + k)),
+                (me - k >= 0, me + k < n_slab, win_copy(t, reach, reach + k, me - k)),
+            )
+        return (
+            (has_r & (me - k + 1 >= 0), me - k >= 0, win_copy(t, reach - k + 1, reach - k, me + 1)),
+            (has_l & (me + k - 1 < n_slab), me + k < n_slab, win_copy(t, reach + k - 1, reach + k, me - 1)),
+        )
+
+    arrived = set()
+
+    def hop_wait(t, k):
+        if k > 0 and (t, k) not in arrived:
+            arrived.add((t, k))
+            for _, receives, copy in sides(t, k):
+                pl.when(receives)(copy.wait_recv)
+
     def hop(t, k):
-        right = win_copy(t, reach - k + 1, reach - k, me + 1)
-        left = win_copy(t, reach + k - 1, reach + k, me - 1)
-        pl.when(has_r & (me - k + 1 >= 0))(lambda: right.start())
-        pl.when(has_l & (me + k - 1 < n_slab))(lambda: left.start())
-
-    def hop_wait(t, k):
-        pl.when(me - k >= 0)(lambda: win_copy(t, reach - k + 1, reach - k, me + 1).wait_recv())
-        pl.when(me + k < n_slab)(lambda: win_copy(t, reach + k - 1, reach + k, me - 1).wait_recv())
+        if t not in DIRECT:
+            hop_wait(t, k - 1)
+        for sends, _, copy in sides(t, k):
+            pl.when(sends)(copy.start)
 
     def hop_done(t, k):
-        pl.when(has_r & (me - k + 1 >= 0))(
-            lambda: win_copy(t, reach - k + 1, reach - k, me + 1).wait_send())
-        pl.when(has_l & (me + k - 1 < n_slab))(
-            lambda: win_copy(t, reach + k - 1, reach + k, me - 1).wait_send())
+        for sends, _, copy in sides(t, k):
+            pl.when(sends)(copy.wait_send)
 
     rho = rho_ref[...]
     vp = vp_ref[...]
@@ -180,7 +206,7 @@
         wf[1, i] = jnp.zeros(wf.shape[2:], F32)
         return carry
 
-    lax.fori_loop(0, STEPS * shots, zero, 0)
+    lax.fori_loop(0, STEPS * shots, zero, 0, unroll=2)
 
     sign_rows = jnp.where(row < shots, DT, -DT)
 
@@ -195,7 +221,7 @@
                 wf[1, t * shots + s, zc, base : base + width, :] = cut[width:]
             return carry
 
-        lax.fori_loop(0, shots, body, 0)
+        lax.fori_loop(0, shots, body, 0, unroll=True)
 
     for t in range(STEPS):
         pl.when(has_l)(lambda: halo_copy(t, True).wait_recv())
@@ -248,58 +274,73 @@
                     win[t, reach, s] = jnp.concatenate([pressure, slide_z - slide_x], 0).astype(BF16)
                 return carry
 
-            lax.fori_loop(0, shots, step, 0)
+            lax.fori_loop(0, shots, step, 0, unroll=True)
         if t < STEPS - 1:
             send_halo(t + 1)
-        hop(t, 1)
+        if t in DIRECT:
+            for k in range(1, reach + 1):
+                hop(t, k)
+        else:
+            hop(t, 1)
         for k in range(2, reach + 1):
-            if t - k + 1 >= 0:
-                hop_wait(t - k + 1, k - 1)
+            if t - k + 1 >= 0 and t - k + 1 not in DIRECT:
                 hop(t - k + 1, k)
         widen(t, reach)
 
-    for late in range(1, reach + 1):
-        for k in range(2, reach + 1):
-            t = STEPS - 1 + late - k + 1
-            if 0 <= t < STEPS:
-                hop_wait(t, k - 1)
-                hop(t, k)
-    for t in range(STEPS):
-        hop_wait(t, reach)
-        for k in range(1, reach + 1):
+    def take(t, low, high):
+        for k in range(low, high + 1):
+            hop_wait(t, k)
             pl.when(me - k >= 0)(functools.partial(widen, t, reach - k))
             pl.when(me + k < n_slab)(functools.partial(widen, t, reach + k))
 
     scale = 1.0 / (shots * n_shot * STEPS)
 
-    def correlate(owner):
+    def correlate(t, owner):
         h0 = pl.multiple_of(owner * per, 8)
 
         def over_z(zc, carry):
-            def over_ts(ts, sums):
-                source = srcf[ts, zc]
-                out = []
+            sums = [None] * (2 * (per + 1))
+            for s in range(shots):
+                source = srcf[t * shots + s, zc]
                 for c in range(2):
                     for p in range(per + 1):
-                        out.append(
-                            sums[c * (per + 1) + p]
-                            + source * wf[c, ts, zc, pl.ds(h0 + p, width), :])
-                return tuple(out)
-
-            sums = lax.fori_loop(
-                0, STEPS * shots, over_ts,
-                tuple(jnp.zeros((width, LANES), F32) for _ in range(2 * (per + 1))), unroll=2)
+                        term = source * wf[c, t * shots + s, zc, pl.ds(h0 + p, width), :]
+                        i = c * (per + 1) + p
+                        sums[i] = term if s == 0 else sums[i] + term
             at = pl.ds(pl.multiple_of(zc * LANES, LANES), LANES)
             for p in range(per):
                 keep = off_ref[h0 + p] == h0 + p - SHIFT
                 both = scale * jnp.concatenate(
                     [jnp.where(keep, sums[c * (per + 1) + p], sums[c * (per + 1) + p + 1])
                      for c in range(2)], 0)
+                if t > 0:
+                    both = both + part[h0 + p, :, at]
                 part[h0 + p, :, at] = both
-                part_bf[h0 + p, :, at] = both.astype(BF16)
+                if t == STEPS - 1:
+                    part_bf[h0 + p, :, at] = both.astype(BF16)
             return carry
 
         lax.fori_loop(0, zc_n, over_z, 0)
+
+    def all_owners(t):
+        def body(owner, carry):
+            correlate(t, owner)
+            return carry
+
+        lax.fori_loop(0, n_shot, body, 0)
+
+    for t in range(STEPS - 1):
+        take(t, 1, reach)
+        all_owners(t)
+        for k in range(2, reach + 1):
+            later = STEPS + t - k + 1
+            if 0 <= later < STEPS and later not in DIRECT:
+                hop(later, k)
+    for late in range(STEPS, STEPS + reach):
+        for k in range(2, reach + 1):
+            later = late + STEPS - 1 - k + 1
+            if 0 <= later < STEPS and later not in DIRECT:
+                hop(later, k)
 
     def r1_copy(a):
         start = (2 * a + 1 - par) * per
@@ -308,34 +349,40 @@
             send_sem=r1_send.at[a], recv_sem=r1_recv.at[a],
             device_id={"shot": mate}, device_id_type=MESH)
 
-    for q in range(1, na + 1):
-        a = lax.rem(mine + q, na)
-        correlate(2 * a + 1 - par)
-        r1_copy(a).start()
-
-    def r2_copy(q):
-        a = lax.rem(mine + q, na)
+    def r2_copy(a):
+        q = lax.rem(a - mine + na, na)
         return pltpu.make_async_remote_copy(
             src_ref=s2.at[q - 1], dst_ref=r2.at[q - 1],
             send_sem=r2_send.at[q - 1], recv_sem=r2_recv.at[q - 1],
             device_id={"shot": 2 * a + par}, device_id_type=MESH)
 
+    last = STEPS - 1
+    near = min(reach, -(-per // width)) if na == 2 else reach
+    take(last, 1, near)
+    for turn in range(na):
+        if turn == 1:
+            take(last, near + 1, reach)
+        ahead = lax.rem(turn + par, na)
+        correlate(last, 2 * ahead + 1 - par)
+        r1_copy(ahead).start()
+        a = lax.rem(turn + 1 - par, na)
+        owner = 2 * a + par
+        correlate(last, owner)
+        r1_copy(a).wait_recv()
+
+        @pl.when(a != mine)
+        def _(a=a, owner=owner):
+            q = lax.rem(a - mine + na, na)
+
+            def join(p, carry):
+                s2[q - 1, p] = (part[owner * per + p] + r1[a, p].astype(F32)).astype(BF16)
+                return carry
+
+            lax.fori_loop(0, per, join, 0, unroll=4)
+            r2_copy(a).start()
+
     for q in range(1, na):
-        a = lax.rem(mine + q, na)
-        owner = 2 * a + par
-        correlate(owner)
-        r1_copy(a).wait_recv()
-
-        def join(p, carry, a=a, owner=owner, q=q):
-            s2[q - 1, p] = (part[owner * per + p] + r1[a, p].astype(F32)).astype(BF16)
-            return carry
-
-        lax.fori_loop(0, per, join, 0)
-        r2_copy(q).start()
-    correlate(shot)
-    r1_copy(mine).wait_recv()
-    for q in range(1, na):
-        r2_copy(q).wait_recv()
+        r2_copy(lax.rem(mine + q, na)).wait_recv()
 
     ratio = vs / vp
     coef = 2.0 * ratio * ratio
@@ -353,7 +400,7 @@
         orho_ref[p] = vp * vp * pp + vs * vs * ps
         return carry
 
-    lax.fori_loop(0, per, finish, 0)
+    lax.fori_loop(0, per, finish, 0, unroll=4)
 
     for t in range(STEPS):
         pl.when(has_r)(lambda: halo_copy(t, True).wait_send())
@@ -365,7 +412,16 @@
     for a in range(na):
         r1_copy(lax.rem(mine + a, na)).wait_send()
     for q in range(1, na):
-        r2_copy(q).wait_send()
+        r2_copy(lax.rem(mine + q, na)).wait_send()
+
+
+def store(*refs):
+    copies = [
+        pltpu.make_async_copy(refs[i], refs[5 + i], refs[10].at[i]) for i in range(5)]
+    for copy in copies:
+        copy.start()
+    for copy in copies:
+        copy.wait()
 
 
 def shards(n_slab, n_shot, source_state, receiver_state, p_velocity, s_velocity, density,
@@ -382,16 +438,26 @@
     nz = depth // LANES
     ts = STEPS * shots
     vmem = pl.BlockSpec(memory_space=pltpu.VMEM)
+    hbm = pl.BlockSpec(memory_space=pltpu.HBM)
     smem = pl.BlockSpec(memory_space=pltpu.SMEM)
     image = jax.ShapeDtypeStruct((per, width, depth), F32)
     state = jax.ShapeDtypeStruct(source_state.shape, F32)
     dma = pltpu.SemaphoreType.DMA
-    return pl.pallas_call(
+    results = pl.pallas_call(
         functools.partial(kernel, n_slab, n_shot, reach, shots, noff),
         out_shape=(state, state, image, image, image),
-        in_specs=[vmem] * 6 + [smem, smem, vmem, vmem, smem],
+        in_specs=[hbm] * 6 + [smem, smem, hbm, hbm, smem],
         out_specs=(vmem,) * 5,
         scratch_shapes=[
+            pltpu.VMEM(source_state.shape, F32),
+            pltpu.VMEM(source_state.shape, F32),
+            pltpu.VMEM((width, depth), F32),
+            pltpu.VMEM((width, depth), F32),
+            pltpu.VMEM((width, depth), F32),
+            pltpu.VMEM(receiver_data.shape, F32),
+            pltpu.VMEM((1, nrec), jnp.int32),
+            pltpu.VMEM((1, nrec), jnp.int32),
+            dma((8,)),
             pltpu.VMEM((4, width, depth), F32),
             pltpu.VMEM((ts * width, depth), F32),
             pltpu.VMEM((ts * width, nrec), F32),
@@ -415,9 +481,16 @@
             dma((na,)), dma((na,)), dma((na - 1,)), dma((na - 1,)),
         ],
         compiler_params=pltpu.CompilerParams(
-            collective_id=0, has_side_effects=True, vmem_limit_bytes=40 * 2**20),
+            collective_id=0, has_side_effects=True, vmem_limit_bytes=61 * 2**20),
     )(source_state, receiver_state, p_velocity, s_velocity, density, receiver_data,
       source_x, source_z, receiver_x.reshape(1, nrec), receiver_z.reshape(1, nrec), offsets)
+    return pl.pallas_call(
+        store,
+        out_shape=(state, state, image, image, image),
+        in_specs=[vmem] * 5,
+        out_specs=(hbm,) * 5,
+        scratch_shapes=[dma((5,))],
+    )(*results)
 
 
 def solution(mesh):

time: 56.6 us -> 47.2 us (0.83)
  local copies, waits for them, and re-layouts: 9.06 us -> 0 us
    unnamed x27 -> x0, local copies, waits for them, and re-layouts: 9.06 us -> none
    pallas_call x0 -> x1, Pallas kernels: none -> 2.44 us  [shards(): pl.pallas_call(store, out_shape=(state, state, image, image, image), in_s...]
    pallas_call x1, Pallas kernels: 46.3 us -> 43.9 us  [shards(): pl.pallas_call(functools.partial(kernel, n_slab, n_shot, reach, shots, no...]
where the time goes in v2:
time: 47.2 us; the launch traced here: 47 us
  Pallas kernels  46.4 us (98%)
  between operations  0.64 us (1%)
    pallas_call x1, Pallas kernels, shards(): pl.pallas_call(functools.partial(kernel, n_slab, n_shot, reach, shots, no...  43.9 us
    pallas_call x1, Pallas kernels, shards(): pl.pallas_call(store, out_shape=(state, state, image, image, image), in_s...  2.44 us

profile of v2, /device:TPU:0, one launch (start us, length us, event | category | flops | bytes accessed | tf_op | source)
XLA Modules:
  0.0 47.0 jit_solution(10270308782129935599)
XLA Ops:
  0.6 43.9 %shard_map.146 = (f32[4,5,8,512]{3,2,1,0:T(8,128)}, f32[4,5,8,512]{3,2,1,0:T(8,128)}, f32[16,8,512]{2,1,0:T(8,128)}, f32[16,8,512]{2,1,0:T(8,128)}, f32[16,8,512]{2,1,0:T(8,128)}) custom-call(f32[4,5,8,512]{3,2,1,0:T(8,128)} %src_in.1, f32[4,5,8,512]{3,2,1,0:T(8,128)} %rec_in.1, f32[8,512]{1,0:T(8,128)} %vp_in.1, f32[8,512]{1,0:T(8,128)} %vs_in.1, ...), custom_call_target="tpu_custom_call" | custom-call | tf_op jit(solution)/shard_map/pallas_call | solution.py:446
  44.6 2.4 %shard_map.147 = (f32[4,5,8,512]{3,2,1,0:T(8,128)}, f32[4,5,8,512]{3,2,1,0:T(8,128)}, f32[16,8,512]{2,1,0:T(8,128)}, f32[16,8,512]{2,1,0:T(8,128)}, f32[16,8,512]{2,1,0:T(8,128)}) custom-call(f32[4,5,8,512]{3,2,1,0:T(8,128)} %get-tuple-element.10.refs_0_, f32[4,5,8,512]{3,2,1,0:T(8,128)} %get-tuple-element.11.refs_1_, ...), custom_call_target="tpu_custom_call" | custom-call | tf_op jit(solution)/shard_map/pallas_call | solution.py:487

commit v3 on v2

--- a/solution.py
+++ b/solution.py
@@ -12,7 +12,6 @@
 SHIFT = 32
 LANES = 128
 DT = 0.3
-DIRECT = ()
 F32 = jnp.float32
 BF16 = jnp.bfloat16
 MESH = pl.DeviceIdType.MESH
@@ -135,11 +134,6 @@
             device_id={"slab": target}, device_id_type=MESH)
 
     def sides(t, k):
-        if t in DIRECT:
-            return (
-                (me + k < n_slab, me - k >= 0, win_copy(t, reach, reach - k, me + k)),
-                (me - k >= 0, me + k < n_slab, win_copy(t, reach, reach + k, me - k)),
-            )
         return (
             (has_r & (me - k + 1 >= 0), me - k >= 0, win_copy(t, reach - k + 1, reach - k, me + 1)),
             (has_l & (me + k - 1 < n_slab), me + k < n_slab, win_copy(t, reach + k - 1, reach + k, me - 1)),
@@ -154,8 +148,7 @@
                 pl.when(receives)(copy.wait_recv)
 
     def hop(t, k):
-        if t not in DIRECT:
-            hop_wait(t, k - 1)
+        hop_wait(t, k - 1)
         for sends, _, copy in sides(t, k):
             pl.when(sends)(copy.start)
 
@@ -204,6 +197,9 @@
     def zero(i, carry):
         wf[0, i] = jnp.zeros(wf.shape[2:], F32)
         wf[1, i] = jnp.zeros(wf.shape[2:], F32)
+        some = pl.ds(i * (noff // (STEPS * shots)), noff // (STEPS * shots))
+        part[some] = jnp.zeros((noff // (STEPS * shots),) + part.shape[1:], F32)
+        part_bf[some] = jnp.zeros((noff // (STEPS * shots),) + part.shape[1:], BF16)
         return carry
 
     lax.fori_loop(0, STEPS * shots, zero, 0, unroll=2)
@@ -222,6 +218,117 @@
             return carry
 
         lax.fori_loop(0, shots, body, 0, unroll=True)
+
+    def take(t, k):
+        hop_wait(t, k)
+        pl.when(me - k >= 0)(functools.partial(widen, t, reach - k))
+        pl.when(me + k < n_slab)(functools.partial(widen, t, reach + k))
+
+    scale = 1.0 / (shots * n_shot * STEPS)
+    last = STEPS - 1
+
+    def correlate(t, group):
+        h0 = pl.multiple_of(group * width, 8)
+        slab = me + group - span
+
+        def over_z(zc, carry):
+            sums = [None] * (2 * (width + 1))
+            for s in range(shots):
+                source = srcf[t * shots + s, zc]
+                for c in range(2):
+                    for p in range(width + 1):
+                        term = source * wf[c, t * shots + s, zc, pl.ds(h0 + p, width), :]
+                        i = c * (width + 1) + p
+                        sums[i] = term if s == 0 else sums[i] + term
+            at = pl.ds(pl.multiple_of(zc * LANES, LANES), LANES)
+            for p in range(width):
+                keep = off_ref[h0 + p] == h0 + p - SHIFT
+                both = scale * jnp.concatenate(
+                    [jnp.where(keep, sums[c * (width + 1) + p], sums[c * (width + 1) + p + 1])
+                     for c in range(2)], 0)
+                if t > 0:
+                    both = both + part[h0 + p, :, at]
+                part[h0 + p, :, at] = both
+                if t == last:
+                    part_bf[h0 + p, :, at] = both.astype(BF16)
+            return carry
+
+        @pl.when((slab + 1 >= 0) & (slab < n_slab))
+        def _():
+            lax.fori_loop(0, zc_n, over_z, 0)
+
+    def pair(t, k):
+        def body(i, carry):
+            correlate(t, span - k + i * (2 * k - 1))
+            return carry
+
+        lax.fori_loop(0, 2, body, 0)
+
+    halves = per // width
+
+    def own_group(k):
+        low, high = span - k, span + k - 1
+        odd = (low // halves) % 2
+        return jnp.where(par == odd, low, high), jnp.where(par == odd, high, low)
+
+    def r1_copy(k):
+        return pltpu.make_async_remote_copy(
+            src_ref=part_bf.at[pl.ds(own_group(k)[1] * width, width)], dst_ref=r1.at[k - 1],
+            send_sem=r1_send.at[k - 1], recv_sem=r1_recv.at[k - 1],
+            device_id={"shot": mate}, device_id_type=MESH)
+
+    def r2_copy(k, q, target):
+        return pltpu.make_async_remote_copy(
+            src_ref=s2.at[k - 1], dst_ref=r2.at[q - 1, k - 1],
+            send_sem=r2_send.at[k - 1], recv_sem=r2_recv.at[q - 1, k - 1],
+            device_id={"shot": target}, device_id_type=MESH)
+
+    def owner_of(k):
+        owner = own_group(k)[0] // halves
+        return owner, lax.rem(owner // 2 - mine + na, na)
+
+    def begin(k):
+        own, other = own_group(k)
+        correlate(last, other)
+        r1_copy(k).start()
+        return own
+
+    def join(k):
+        r1_copy(k).wait_recv()
+        owner, q = owner_of(k)
+        own = own_group(k)[0]
+
+        @pl.when(owner != shot)
+        def _():
+            def body(p, carry):
+                s2[k - 1, p] = (part[own * width + p] + r1[k - 1, p].astype(F32)).astype(BF16)
+                return carry
+
+            lax.fori_loop(0, width, body, 0, unroll=True)
+            r2_copy(k, q, owner).start()
+
+    def advance(v):
+        for k in range(2, reach + 1):
+            if 0 <= v - k + 1 <= last:
+                hop(v - k + 1, k)
+        levels = []
+        for k in range(1, span + 1):
+            t = v - min(k, reach)
+            if 0 <= t <= last:
+                if k <= reach:
+                    take(t, k)
+                if t == last:
+                    levels.append(k)
+                else:
+                    pair(t, k)
+        for k in levels:
+            begin(k)
+        if v - 1 > last:
+            for k in range(1, span + 1):
+                if v - 1 - min(k, reach) == last:
+                    join(k)
+        for k in levels:
+            correlate(last, own_group(k)[0])
 
     for t in range(STEPS):
         pl.when(has_l)(lambda: halo_copy(t, True).wait_recv())
@@ -277,130 +384,41 @@
             lax.fori_loop(0, shots, step, 0, unroll=True)
         if t < STEPS - 1:
             send_halo(t + 1)
-        if t in DIRECT:
-            for k in range(1, reach + 1):
-                hop(t, k)
-        else:
-            hop(t, 1)
-        for k in range(2, reach + 1):
-            if t - k + 1 >= 0 and t - k + 1 not in DIRECT:
-                hop(t - k + 1, k)
+        hop(t, 1)
         widen(t, reach)
-
-    def take(t, low, high):
-        for k in range(low, high + 1):
-            hop_wait(t, k)
-            pl.when(me - k >= 0)(functools.partial(widen, t, reach - k))
-            pl.when(me + k < n_slab)(functools.partial(widen, t, reach + k))
-
-    scale = 1.0 / (shots * n_shot * STEPS)
-
-    def correlate(t, owner):
-        h0 = pl.multiple_of(owner * per, 8)
-
-        def over_z(zc, carry):
-            sums = [None] * (2 * (per + 1))
-            for s in range(shots):
-                source = srcf[t * shots + s, zc]
-                for c in range(2):
-                    for p in range(per + 1):
-                        term = source * wf[c, t * shots + s, zc, pl.ds(h0 + p, width), :]
-                        i = c * (per + 1) + p
-                        sums[i] = term if s == 0 else sums[i] + term
-            at = pl.ds(pl.multiple_of(zc * LANES, LANES), LANES)
-            for p in range(per):
-                keep = off_ref[h0 + p] == h0 + p - SHIFT
-                both = scale * jnp.concatenate(
-                    [jnp.where(keep, sums[c * (per + 1) + p], sums[c * (per + 1) + p + 1])
-                     for c in range(2)], 0)
-                if t > 0:
-                    both = both + part[h0 + p, :, at]
-                part[h0 + p, :, at] = both
-                if t == STEPS - 1:
-                    part_bf[h0 + p, :, at] = both.astype(BF16)
-            return carry
-
-        lax.fori_loop(0, zc_n, over_z, 0)
-
-    def all_owners(t):
-        def body(owner, carry):
-            correlate(t, owner)
-            return carry
-
-        lax.fori_loop(0, n_shot, body, 0)
-
-    for t in range(STEPS - 1):
-        take(t, 1, reach)
-        all_owners(t)
-        for k in range(2, reach + 1):
-            later = STEPS + t - k + 1
-            if 0 <= later < STEPS and later not in DIRECT:
-                hop(later, k)
-    for late in range(STEPS, STEPS + reach):
-        for k in range(2, reach + 1):
-            later = late + STEPS - 1 - k + 1
-            if 0 <= later < STEPS and later not in DIRECT:
-                hop(later, k)
-
-    def r1_copy(a):
-        start = (2 * a + 1 - par) * per
-        return pltpu.make_async_remote_copy(
-            src_ref=part_bf.at[pl.ds(start, per)], dst_ref=r1.at[a],
-            send_sem=r1_send.at[a], recv_sem=r1_recv.at[a],
-            device_id={"shot": mate}, device_id_type=MESH)
-
-    def r2_copy(a):
-        q = lax.rem(a - mine + na, na)
-        return pltpu.make_async_remote_copy(
-            src_ref=s2.at[q - 1], dst_ref=r2.at[q - 1],
-            send_sem=r2_send.at[q - 1], recv_sem=r2_recv.at[q - 1],
-            device_id={"shot": 2 * a + par}, device_id_type=MESH)
-
-    last = STEPS - 1
-    near = min(reach, -(-per // width)) if na == 2 else reach
-    take(last, 1, near)
-    for turn in range(na):
-        if turn == 1:
-            take(last, near + 1, reach)
-        ahead = lax.rem(turn + par, na)
-        correlate(last, 2 * ahead + 1 - par)
-        r1_copy(ahead).start()
-        a = lax.rem(turn + 1 - par, na)
-        owner = 2 * a + par
-        correlate(last, owner)
-        r1_copy(a).wait_recv()
-
-        @pl.when(a != mine)
-        def _(a=a, owner=owner):
-            q = lax.rem(a - mine + na, na)
-
-            def join(p, carry):
-                s2[q - 1, p] = (part[owner * per + p] + r1[a, p].astype(F32)).astype(BF16)
-                return carry
-
-            lax.fori_loop(0, per, join, 0, unroll=4)
-            r2_copy(a).start()
-
-    for q in range(1, na):
-        r2_copy(lax.rem(mine + q, na)).wait_recv()
+        advance(t)
+
+    for v in range(STEPS, STEPS + reach):
+        advance(v)
+    for k in range(reach, span + 1):
+        join(k)
 
     ratio = vs / vp
     coef = 2.0 * ratio * ratio
     rho_vp = 2.0 * rho * vp
     rho_vs = 2.0 * rho * vs
 
-    def finish(p, carry):
-        both = part[shot * per + p] + r1[mine, p].astype(F32)
+    for half in range(halves):
+        group = shot * halves + half
+        level = jnp.where(group < span, span - group - 1, group - span)
         for q in range(1, na):
-            both = both + r2[q - 1, p].astype(F32)
-        pp = both[:width]
-        ps = both[width:]
-        ovp_ref[p] = rho_vp * pp
-        ovs_ref[p] = rho_vs * (ps - coef * pp)
-        orho_ref[p] = vp * vp * pp + vs * vs * ps
-        return carry
-
-    lax.fori_loop(0, per, finish, 0, unroll=4)
+            pltpu.make_async_remote_copy(
+                src_ref=s2.at[level], dst_ref=r2.at[na - q - 1, level],
+                send_sem=r2_send.at[level], recv_sem=r2_recv.at[q - 1, level],
+                device_id={"shot": mate}, device_id_type=MESH).wait_recv()
+
+        def finish(p, carry, half=half, group=group, level=level):
+            both = part[group * width + p] + r1[level, p].astype(F32)
+            for q in range(1, na):
+                both = both + r2[q - 1, level, p].astype(F32)
+            pp = both[:width]
+            ps = both[width:]
+            ovp_ref[half * width + p] = rho_vp * pp
+            ovs_ref[half * width + p] = rho_vs * (ps - coef * pp)
+            orho_ref[half * width + p] = vp * vp * pp + vs * vs * ps
+            return carry
+
+        lax.fori_loop(0, width, finish, 0, unroll=True)
 
     for t in range(STEPS):
         pl.when(has_r)(lambda: halo_copy(t, True).wait_send())
@@ -409,10 +427,10 @@
             hop_done(t, k)
     pl.when(has_r)(lambda: rho_copy(True).wait_send())
     pl.when(has_l)(lambda: rho_copy(False).wait_send())
-    for a in range(na):
-        r1_copy(lax.rem(mine + a, na)).wait_send()
-    for q in range(1, na):
-        r2_copy(lax.rem(mine + q, na)).wait_send()
+    for k in range(1, span + 1):
+        r1_copy(k).wait_send()
+        owner, q = owner_of(k)
+        pl.when(owner != shot)(r2_copy(k, q, owner).wait_send)
 
 
 def store(*refs):
@@ -473,12 +491,12 @@
             pltpu.VMEM((2, ts, nz, (2 * span + 1) * width, LANES), F32),
             pltpu.VMEM((noff, 2 * width, depth), F32),
             pltpu.VMEM((noff, 2 * width, depth), BF16),
-            pltpu.VMEM((na, per, 2 * width, depth), BF16),
-            pltpu.VMEM((na - 1, per, 2 * width, depth), BF16),
-            pltpu.VMEM((na - 1, per, 2 * width, depth), BF16),
+            pltpu.VMEM((span, width, 2 * width, depth), BF16),
+            pltpu.VMEM((span, width, 2 * width, depth), BF16),
+            pltpu.VMEM((na - 1, span, width, 2 * width, depth), BF16),
             dma((STEPS, 2)), dma((STEPS, 2)), dma((2,)), dma((2,)),
             dma((STEPS, slots)), dma((STEPS, slots)),
-            dma((na,)), dma((na,)), dma((na - 1,)), dma((na - 1,)),
+            dma((span,)), dma((span,)), dma((span,)), dma((na - 1, span)),
         ],
         compiler_params=pltpu.CompilerParams(
             collective_id=0, has_side_effects=True, vmem_limit_bytes=61 * 2**20),

time: 47.2 us -> 44.3 us (0.939)
  Pallas kernels: 46.4 us -> 43.5 us
    pallas_call x1, Pallas kernels: 43.9 us -> 41 us  [shards(): pl.pallas_call(functools.partial(kernel, n_slab, n_shot, reach, shots, no...]
where the time goes in v3:
time: 44.3 us; the launch traced here: 44.1 us
  Pallas kernels  43.5 us (98%)
  between operations  0.64 us (1%)
    pallas_call x1, Pallas kernels, shards(): pl.pallas_call(functools.partial(kernel, n_slab, n_shot, reach, shots, no...  41 us
    pallas_call x1, Pallas kernels, shards(): pl.pallas_call(store, out_shape=(state, state, image, image, image), in_s...  2.44 us

profile of v3, /device:TPU:0, one launch (start us, length us, event | category | flops | bytes accessed | tf_op | source)
XLA Modules:
  0.0 44.1 jit_solution(16009191383732205711)
XLA Ops:
  0.6 41.0 %shard_map.146 = (f32[4,5,8,512]{3,2,1,0:T(8,128)}, f32[4,5,8,512]{3,2,1,0:T(8,128)}, f32[16,8,512]{2,1,0:T(8,128)}, f32[16,8,512]{2,1,0:T(8,128)}, f32[16,8,512]{2,1,0:T(8,128)}) custom-call(f32[4,5,8,512]{3,2,1,0:T(8,128)} %src_in.1, f32[4,5,8,512]{3,2,1,0:T(8,128)} %rec_in.1, f32[8,512]{1,0:T(8,128)} %vp_in.1, f32[8,512]{1,0:T(8,128)} %vs_in.1, ...), custom_call_target="tpu_custom_call" | custom-call | tf_op jit(solution)/shard_map/pallas_call | solution.py:464
  41.7 2.4 %shard_map.147 = (f32[4,5,8,512]{3,2,1,0:T(8,128)}, f32[4,5,8,512]{3,2,1,0:T(8,128)}, f32[16,8,512]{2,1,0:T(8,128)}, f32[16,8,512]{2,1,0:T(8,128)}, f32[16,8,512]{2,1,0:T(8,128)}) custom-call(f32[4,5,8,512]{3,2,1,0:T(8,128)} %get-tuple-element.10.refs_0_, f32[4,5,8,512]{3,2,1,0:T(8,128)} %get-tuple-element.11.refs_1_, ...), custom_call_target="tpu_custom_call" | custom-call | tf_op jit(solution)/shard_map/pallas_call | solution.py:505
